TPU v7x, 32 devices: a whole 2x2x4 slice. The times are simulated.
32 devices in a mesh: dp: 4 (over z), ctx: 4 (over x, core), tensor: 2 (over y).
Axes of the slice: x: 2, y: 2, z: 4, core: 2. Of those that a mesh axis runs over, the one named last changes fastest.
Arguments:
- tokens: bfloat16 [8192, 768], P(('dp', 'ctx')), may hold values from -6 to 6
- out_grad: bfloat16 [8192, 768], P(('dp', 'ctx')), may hold values from -6 to 6
- lengths: int32 [4, 3], P('dp'), may hold values from 1 to 1024, 2048 in all within a row
- query_weight: bfloat16 [768, 768], P(None, 'tensor'), may hold values from -0.21875 to 0.21875
- query_bias: float32 [768], P('tensor'), may hold values from -3 to 3
- key_weight: bfloat16 [768, 768], P(None, 'tensor'), may hold values from -0.21875 to 0.21875
- key_bias: float32 [768], P('tensor'), may hold values from -3 to 3
- value_weight: bfloat16 [768, 768], P(None, 'tensor'), may hold values from -0.21875 to 0.21875
- value_bias: float32 [768], P('tensor'), may hold values from -3 to 3
- output_weight: bfloat16 [768, 768], P('tensor'), may hold values from -0.875 to 0.875
- output_bias: float32 [768], replicated, may hold values from -3 to 3
- first_gain: float32 [768], replicated, may hold values from 0.5 to 1.5
- first_shift: float32 [768], replicated, may hold values from -3 to 3
- inner_weight: bfloat16 [768, 3072], P(None, 'tensor'), may hold values from -0.21875 to 0.21875
- inner_bias: float32 [3072], P('tensor'), may hold values from -3 to 3
- outer_weight: bfloat16 [3072, 768], P('tensor'), may hold values from -0.109375 to 0.109375
- outer_bias: float32 [768], replicated, may hold values from -3 to 3
- second_gain: float32 [768], replicated, may hold values from 0.5 to 1.5
- second_shift: float32 [768], replicated, may hold values from -3 to 3
Outputs:
- layer_out: bfloat16 [8192, 768], P(('dp', 'ctx'))
- input_grad: bfloat16 [8192, 768], P(('dp', 'ctx'))
- query_weight_grad: float32 [768, 768], P(None, 'tensor')
- query_bias_grad: float32 [768], P('tensor')
- key_weight_grad: float32 [768, 768], P(None, 'tensor')
- key_bias_grad: float32 [768], P('tensor')
- value_weight_grad: float32 [768, 768], P(None, 'tensor')
- value_bias_grad: float32 [768], P('tensor')
- output_weight_grad: float32 [768, 768], P('tensor')
- output_bias_grad: float32 [768], replicated
- first_gain_grad: float32 [768], replicated
- first_shift_grad: float32 [768], replicated
- inner_weight_grad: float32 [768, 3072], P(None, 'tensor')
- inner_bias_grad: float32 [3072], P('tensor')
- outer_weight_grad: float32 [3072, 768], P('tensor')
- outer_bias_grad: float32 [768], replicated
- second_gain_grad: float32 [768], replicated
- second_shift_grad: float32 [768], replicated
Inputs may be any that keep to these rules, and one draw needn't show every extreme that they name: Row g holds the lengths of the 3 sequences of data group g in order; they sum to 2048 and the longest is 1024.
All inputs are finite; a program needn't handle non-finite values.
Results may differ from a plain program's by a relative error of at most 0.03.
Values may be sent and summed in bfloat16 or wider, within the bound.
No kernel may reach another device: no remote copies, remote signals or barrier semaphores. Data moves between devices by JAX's collectives and lax.ppermute only.
A program may use at most 128 MiB of HBM per device.

v0:
```python
import jax
import jax.numpy as jnp
from jax import lax
from jax.sharding import PartitionSpec as P

HEAD_DIM = 64


MASKED = -1e30
EPSILON = 1e-06


def rope_tables(position, head_width):
    half_dim = head_width // 2
    frequency = jnp.power(10000.0, -2.0 * jnp.arange(half_dim, dtype=jnp.float32) / head_width)
    angles = position.astype(jnp.float32)[:, None] * frequency[None, :]
    return (jnp.cos(angles), jnp.sin(angles))


def rotate(vector, cosine_table, sine_table):
    half_dim = vector.shape[-1] // 2
    front_half = vector[..., :half_dim]
    back_half = vector[..., half_dim:]
    cosine = cosine_table[:, None, :]
    sine_part = sine_table[:, None, :]
    return jnp.concatenate(
        [front_half * cosine - back_half * sine_part, front_half * sine_part + back_half * cosine],
        axis=-1,
    )


def rotate_back(gradient, cosine_table, sine_table):
    half_dim = gradient.shape[-1] // 2
    front_half = gradient[..., :half_dim]
    back_half = gradient[..., half_dim:]
    cosine = cosine_table[:, None, :]
    sine_part = sine_table[:, None, :]
    return jnp.concatenate(
        [front_half * cosine + back_half * sine_part, back_half * cosine - front_half * sine_part],
        axis=-1,
    )


def layout(lengths_row, row_index):
    ends = jnp.cumsum(lengths_row)
    starts = ends - lengths_row
    segment = jnp.sum((row_index[:, None] >= ends[None, :]).astype(jnp.int32), axis=1)
    member = segment[:, None] == jnp.arange(lengths_row.shape[0], dtype=jnp.int32)[None, :]
    position = row_index - jnp.sum(jnp.where(member, starts[None, :], 0), axis=1)
    return (segment, position)


def normalize(rows_in):
    row_mean = jnp.mean(rows_in, axis=-1, keepdims=True)
    centered = rows_in - row_mean
    inverse = lax.rsqrt(jnp.mean(centered * centered, axis=-1, keepdims=True) + EPSILON)
    return (centered * inverse, inverse)


def norm_back(grad_normed, normed, inverse):
    return inverse * (
        grad_normed
        - jnp.mean(grad_normed, axis=-1, keepdims=True)
        - normed * jnp.mean(grad_normed * normed, axis=-1, keepdims=True)
    )


def matmul(left_side, right_side):
    return jnp.dot(left_side, right_side, preferred_element_type=jnp.float32)


def left_contract(left_side, right_side):
    return jnp.einsum("ti,tj->ij", left_side, right_side, preferred_element_type=jnp.float32)


def right_contract(left_side, right_side):
    return jnp.einsum("ti,ji->tj", left_side, right_side, preferred_element_type=jnp.float32)


def column_sums(gradient):
    return jnp.sum(gradient.astype(jnp.float32), axis=0)


def pair_terms(query_block, grad_block, log_block, dot_block, key_piece, value_piece, allowed):
    scores = (
        jnp.einsum("qhd,khd->hqk", query_block, key_piece, preferred_element_type=jnp.float32)
        * 0.125
    )
    attn_prob = jnp.where(allowed, jnp.exp(scores - log_block[..., None]), 0.0)
    prob_grad = jnp.einsum(
        "qhd,khd->hqk", grad_block, value_piece, preferred_element_type=jnp.float32
    )
    score_grad = (attn_prob * (prob_grad - dot_block[..., None])).astype(jnp.bfloat16)
    return (score_grad, attn_prob.astype(jnp.bfloat16))


def per_device(
    tokens,
    out_grad,
    lengths,
    query_weight,
    query_bias,
    key_weight,
    key_bias,
    value_weight,
    value_bias,
    output_weight,
    output_bias,
    first_gain,
    first_shift,
    inner_weight,
    inner_bias,
    outer_weight,
    outer_bias,
    second_gain,
    second_shift,
):
    rows, width = tokens.shape
    heads_here = query_weight.shape[1] // HEAD_DIM
    local_width = heads_here * HEAD_DIM
    span = lax.axis_size("ctx") * rows
    offset = lax.axis_index("ctx") * rows
    last_row = offset + rows - 1
    lengths_row = lengths[0]
    local_index = offset + jnp.arange(rows, dtype=jnp.int32)
    local_segment, local_position = layout(lengths_row, local_index)
    cosine_table, sine_table = rope_tables(local_position, HEAD_DIM)
    query_pre = (matmul(tokens, query_weight) + query_bias).reshape(rows, heads_here, HEAD_DIM)
    key_pre = (matmul(tokens, key_weight) + key_bias).reshape(rows, heads_here, HEAD_DIM)
    value_pre = matmul(tokens, value_weight) + value_bias
    queries = rotate(query_pre, cosine_table, sine_table).astype(jnp.bfloat16)
    key_flat = (
        rotate(key_pre, cosine_table, sine_table).astype(jnp.bfloat16).reshape(rows, local_width)
    )
    value_flat = value_pre.astype(jnp.bfloat16)
    block_rows = min(512, span)
    block_count = span // block_rows

    def allowed_pairs(key_index):
        key_segment, unused = layout(lengths_row, key_index)
        return (local_segment[:, None] == key_segment[None, :]) & (
            key_index[None, :] <= local_index[:, None]
        )

    initial = (
        jnp.full((heads_here, rows), MASKED, jnp.float32),
        jnp.zeros((heads_here, rows), jnp.float32),
        jnp.zeros((rows, heads_here, HEAD_DIM), jnp.float32),
    )
    pieces = (
        lax.all_gather(key_flat, "ctx", axis=0, tiled=True),
        lax.all_gather(value_flat, "ctx", axis=0, tiled=True),
    )

    def attend_compute(carry):
        max_run, total_run, accum = carry
        key_piece = pieces[0].reshape(-1, heads_here, HEAD_DIM)
        value_piece = pieces[1].reshape(-1, heads_here, HEAD_DIM)
        key_index = jnp.arange(key_piece.shape[0], dtype=jnp.int32)
        allowed = allowed_pairs(key_index)[None]
        scores = (
            jnp.einsum("qhd,khd->hqk", queries, key_piece, preferred_element_type=jnp.float32)
            * 0.125
        )
        scores = jnp.where(allowed, scores, MASKED)
        max_new = jnp.maximum(max_run, jnp.max(scores, axis=-1))
        attn_prob = jnp.where(allowed, jnp.exp(scores - max_new[..., None]), 0.0)
        total_new = jnp.sum(attn_prob, axis=-1)
        accum = jnp.einsum(
            "hqk,khd->qhd",
            attn_prob.astype(jnp.bfloat16),
            value_piece,
            preferred_element_type=jnp.float32,
        )
        return (max_new, total_new, accum)

    folded = lax.cond(jnp.int32(0) <= last_row, attend_compute, lambda carry: carry, initial)
    max_run, total_run, accum = folded
    attended = accum / jnp.transpose(total_run)[..., None]
    log_total = max_run + jnp.log(total_run)
    attended_low = attended.reshape(rows, local_width).astype(jnp.bfloat16)
    attn_out = (
        lax.psum(matmul(attended_low, output_weight).astype(jnp.bfloat16), "tensor").astype(
            jnp.float32
        )
        + output_bias
    )
    normed_first, inverse_first = normalize(tokens.astype(jnp.float32) + attn_out)
    first = normed_first * first_gain + first_shift
    first_low = first.astype(jnp.bfloat16)
    pre_act = matmul(first_low, inner_weight) + inner_bias
    hidden = jax.nn.gelu(pre_act, approximate=False).astype(jnp.bfloat16)
    ffn = (
        lax.psum(matmul(hidden, outer_weight).astype(jnp.bfloat16), "tensor").astype(jnp.float32)
        + outer_bias
    )
    normed_second, inverse_second = normalize(first + ffn)
    layer_out = (normed_second * second_gain + second_shift).astype(jnp.bfloat16)
    upstream = out_grad.astype(jnp.float32)
    second_gain_grad = jnp.sum(upstream * normed_second, axis=0)
    second_shift_grad = jnp.sum(upstream, axis=0)
    res2_grad = norm_back(upstream * second_gain, normed_second, inverse_second)
    ffn_grad = res2_grad.astype(jnp.bfloat16)
    outer_bias_grad = column_sums(ffn_grad)
    outer_weight_grad = left_contract(hidden, ffn_grad)
    hidden_grad = right_contract(ffn_grad, outer_weight)
    unused_value, gelu_back = jax.vjp(lambda inner: jax.nn.gelu(inner, approximate=False), pre_act)
    pre_grad = gelu_back(hidden_grad)[0].astype(jnp.bfloat16)
    inner_bias_grad = column_sums(pre_grad)
    inner_weight_grad = left_contract(first_low, pre_grad)
    first_grad = res2_grad + lax.psum(
        right_contract(pre_grad, inner_weight).astype(jnp.bfloat16), "tensor"
    ).astype(jnp.float32)
    first_gain_grad = jnp.sum(first_grad * normed_first, axis=0)
    first_shift_grad = jnp.sum(first_grad, axis=0)
    res1_grad = norm_back(first_grad * first_gain, normed_first, inverse_first)
    attn_grad = res1_grad.astype(jnp.bfloat16)
    output_bias_grad = column_sums(attn_grad)
    output_weight_grad = left_contract(attended_low, attn_grad)
    head_grad = (
        right_contract(attn_grad, output_weight)
        .reshape(rows, heads_here, HEAD_DIM)
        .astype(jnp.bfloat16)
    )
    row_dot = jnp.transpose(jnp.sum(head_grad.astype(jnp.float32) * attended, axis=-1))
    again = (
        lax.all_gather(key_flat, "ctx", axis=0, tiled=True),
        lax.all_gather(value_flat, "ctx", axis=0, tiled=True),
    )
    back_keys = again[0].reshape(block_count, block_rows, heads_here, HEAD_DIM)
    back_values = again[1].reshape(block_count, block_rows, heads_here, HEAD_DIM)
    back_firsts = jnp.arange(block_count, dtype=jnp.int32) * block_rows
    zero_accum = jnp.zeros((rows, heads_here, HEAD_DIM), jnp.float32)

    def back_block(query_accum, inputs):
        key_piece, value_piece, first_row = inputs

        def back_compute(acc):
            key_index = first_row + jnp.arange(block_rows, dtype=jnp.int32)
            allowed = allowed_pairs(key_index)[None]
            score_grad, prob_low = pair_terms(
                queries, head_grad, log_total, row_dot, key_piece, value_piece, allowed
            )
            acc = (
                acc
                + jnp.einsum(
                    "hqk,khd->qhd", score_grad, key_piece, preferred_element_type=jnp.float32
                )
                * 0.125
            )
            key_part = (
                jnp.einsum("hqk,qhd->khd", score_grad, queries, preferred_element_type=jnp.float32)
                * 0.125
            )
            value_part = jnp.einsum(
                "hqk,qhd->khd", prob_low, head_grad, preferred_element_type=jnp.float32
            )
            return (
                acc,
                (
                    key_part.reshape(block_rows, local_width),
                    value_part.reshape(block_rows, local_width),
                ),
            )

        def skip(acc):
            blank = jnp.zeros((block_rows, local_width), jnp.float32)
            return (acc, (blank, blank))

        return lax.cond(first_row <= last_row, back_compute, skip, query_accum)

    query_turned, stacked_parts = lax.scan(
        back_block, zero_accum, (back_keys, back_values, back_firsts)
    )
    key_terms = stacked_parts[0].reshape(span, local_width)
    value_terms = stacked_parts[1].reshape(span, local_width)
    key_turned, value_sum = (
        lax.psum_scatter(
            key_terms.astype(jnp.bfloat16), "ctx", scatter_dimension=0, tiled=True
        ).astype(jnp.float32),
        lax.psum_scatter(
            value_terms.astype(jnp.bfloat16), "ctx", scatter_dimension=0, tiled=True
        ).astype(jnp.float32),
    )
    query_grad = (
        rotate_back(query_turned, cosine_table, sine_table)
        .reshape(rows, local_width)
        .astype(jnp.bfloat16)
    )
    key_grad = (
        rotate_back(key_turned.reshape(rows, heads_here, HEAD_DIM), cosine_table, sine_table)
        .reshape(rows, local_width)
        .astype(jnp.bfloat16)
    )
    value_grad = value_sum.astype(jnp.bfloat16)
    query_bias_grad = column_sums(query_grad)
    key_bias_grad = column_sums(key_grad)
    value_bias_grad = column_sums(value_grad)
    query_weight_grad = left_contract(tokens, query_grad)
    key_weight_grad = left_contract(tokens, key_grad)
    value_weight_grad = left_contract(tokens, value_grad)
    input_part = (
        right_contract(query_grad, query_weight)
        + right_contract(key_grad, key_weight)
        + right_contract(value_grad, value_weight)
    )
    input_grad = (
        res1_grad + lax.psum(input_part.astype(jnp.bfloat16), "tensor").astype(jnp.float32)
    ).astype(jnp.bfloat16)
    summed = lax.psum(
        (
            query_weight_grad,
            query_bias_grad,
            key_weight_grad,
            key_bias_grad,
            value_weight_grad,
            value_bias_grad,
            output_weight_grad,
            output_bias_grad,
            first_gain_grad,
            first_shift_grad,
            inner_weight_grad,
            inner_bias_grad,
            outer_weight_grad,
            outer_bias_grad,
            second_gain_grad,
            second_shift_grad,
        ),
        ("dp", "ctx"),
    )
    return (
        layer_out,
        input_grad,
        summed[0],
        summed[1],
        summed[2],
        summed[3],
        summed[4],
        summed[5],
        summed[6],
        summed[7],
        summed[8],
        summed[9],
        summed[10],
        summed[11],
        summed[12],
        summed[13],
        summed[14],
        summed[15],
    )


def solution(mesh):
    return jax.shard_map(
        per_device,
        mesh=mesh,
        in_specs=(
            P(("dp", "ctx"), None),
            P(("dp", "ctx"), None),
            P("dp", None),
            P(None, "tensor"),
            P("tensor"),
            P(None, "tensor"),
            P("tensor"),
            P(None, "tensor"),
            P("tensor"),
            P("tensor", None),
            P(),
            P(),
            P(),
            P(None, "tensor"),
            P("tensor"),
            P("tensor", None),
            P(),
            P(),
            P(),
        ),
        out_specs=(
            P(("dp", "ctx"), None),
            P(("dp", "ctx"), None),
            P(None, "tensor"),
            P("tensor"),
            P(None, "tensor"),
            P("tensor"),
            P(None, "tensor"),
            P("tensor"),
            P("tensor", None),
            P(),
            P(),
            P(),
            P(None, "tensor"),
            P("tensor"),
            P("tensor", None),
            P(),
            P(),
            P(),
        ),
        check_vma=False,
    )
```

profile of v0, /device:TPU:0, one launch (start us, length us, event | category | flops | bytes accessed | tf_op | source)
XLA Modules:
  0.0 712.8 jit_solution(782877473018015571)
XLA Ops:
  9.5 1.9 convolution_add_fusion.2
  13.8 2.4 fusion.48
  17.4 18.9 %all-gather.3.cloned.1.call-done = bf16[2048,384]{0,1:T(8,128)(2,1)} async-done(((bf16[512,384]{0,1:T(8,128)(2,1)}), bf16[2048,384]{0,1:T(8,128)(2,1)}) %all-gather.3.cloned.1.call-update) | async-done | bytes 1572880 | tf_op jit(solution)/shard_map/all_gather | solution.py:151
  36.3 21.8 %all-gather.5.cloned.1.call-done = bf16[2048,384]{1,0:T(8,128)(2,1)} async-done(((bf16[512,384]{1,0:T(8,128)(2,1)}), bf16[2048,384]{1,0:T(8,128)(2,1)}) %all-gather.5.cloned.1.call-update) | async-done | bytes 1572880 | tf_op jit(solution)/shard_map/all_gather | solution.py:152
  58.1 44.4 %conditional.2 = (f32[6,512]{1,0:T(8,128)}, f32[6,512]{1,0:T(8,128)}, f32[512,6,64]{0,2,1:T(8,128)}, f32[6,512]{1,0:T(8,128)S(1)}) conditional(s32[]{:T(128)} %convert_element_type.162, () %tuple.38, (s32[512]{0:T(512)S(1)}, s32[3]{0:T(128)}, s32[512]{0:T(512)S(1)}, bf16[2048,384]{0,1:T(8,128)(2,1)}, bf16[512,6,64]{0,2,1:T(8,128)(2,1)S(1)}, ...), branch_computations={%region_3.4_spmd, %region_4.9_spmd} | conditional | flops 1695560704 | bytes 91476064 | solution.py:177
  59.0 1.2 fusion.8
  60.3 12.5 %fusion.2 = (f32[6,512]{1,0:T(8,128)S(1)}, f32[6,512,2048]{2,1,0:T(8,128)}) fusion(pred[512,2048]{1,0:T(8,128)(4,1)S(1)} %fusion.8, bf16[512,6,64]{0,2,1:T(8,128)(2,1)S(1)} %get-tuple-element.162, bf16[2048,6,64]{0,2,1:T(8,128)(2,1)} %bitcast.114), kind=kOutput, calls=%fused_computation.3 | convolution fusion | flops 824177664 | bytes 28192768 | tf_op jit(solution)/shard_map/cond/branch_1_fun/qhd,khd->hqk/dot_general | solution.py:162
  73.4 13.2 %fusion.4 = f32[6,512]{1,0:T(8,128)} fusion(f32[6,512,2048]{2,1,0:T(8,128)} %get-tuple-element.489, f32[6,512]{1,0:T(8,128)} %broadcast_maximum_fusion, pred[512,2048]{1,0:T(8,128)(4,1)S(1)} %fusion.8), kind=kLoop, calls=%fused_computation.5 | loop fusion | flops 31454208 | bytes 26238976 | tf_op jit(solution)/shard_map/cond/branch_1_fun/reduce_sum | solution.py:168
  86.5 2.6 copy.75
  89.1 12.7 %fusion.9 = f32[512,6,64]{0,2,1:T(8,128)} fusion(bf16[2048,6,64]{0,2,1:T(8,128)(2,1)} %bitcast.126, f32[6,512,2048]{2,1,0:T(8,128)} %get-tuple-element.489, f32[6,512]{1,0:T(8,128)} %broadcast_maximum_fusion, pred[512,2048]{1,0:T(8,128)(4,1)} %copy-done.13), kind=kOutput, calls=%fused_computation.10 | convolution fusion | flops 836763648 | bytes 28585984 | tf_op jit(solution)/shard_map/cond/branch_1_fun/hqk,khd->qhd/dot_general | solution.py:169
  103.2 1.2 fusion.50
  105.1 2.5 convolution_convert_fusion.2
  107.9 34.2 %all-reduce.8.cloned.1.call-done = bf16[512,768]{1,0:T(8,128)(2,1)} async-done(((bf16[512,768]{1,0:T(8,128)(2,1)}), bf16[512,768]{1,0:T(8,128)(2,1)}) %all-reduce.8.cloned.1.call-update) | async-done | bytes 786448 | tf_op jit(solution)/shard_map/psum | solution.py:183
  142.2 1.5 fusion.49
  144.3 10.3 %multiply_convert_fusion = (bf16[512,1536]{1,0:T(8,128)(2,1)S(1)}, f32[512,1536]{1,0:T(8,128)}, f32[512,1536]{1,0:T(8,128)}) fusion(f32[1536]{0:T(1024)S(1)} %copy-done.51, bf16[768,1536]{1,0:T(8,128)(2,1)S(1)} %copy-done, f32[768]{0:T(1024)} %param.37, f32[768]{0:T(1024)S(1)} %copy-done.35, f32[512]{0:T(512)S(1)} %add_rsqrt_fusion.1, ...), kind=kOutput, calls=%fused_computation.50 | convolution fusion | flops 1263403008 | bytes 11815936 | tf_op jit(solution)/shard_map/dot_general | solution.py:69
  154.6 1.1 copy-done.20
  155.8 2.3 convolution_convert_fusion.1
  158.1 34.4 %all-reduce.10.cloned.1.call-done = bf16[512,768]{1,0:T(8,128)(2,1)} async-done(((bf16[512,768]{1,0:T(8,128)(2,1)}), bf16[512,768]{1,0:T(8,128)(2,1)}) %all-reduce.10.cloned.1.call-update) | async-done | bytes 786448 | tf_op jit(solution)/shard_map/psum | solution.py:194
  192.5 2.3 fusion.65
  196.0 1.3 fusion.46
  197.3 1.5 fusion.44
  199.3 2.9 convert_reduce_fusion.2
  202.2 1.2 copy-done.54
  203.4 2.3 convolution_convert_fusion
  206.6 3.8 reshape.378
  210.5 3.2 copy.77
  213.6 1.6 copy.76
  215.3 3.9 reshape.379
  219.1 3.0 copy.78
  222.2 1.3 add.225
  223.5 16.7 %all-reduce.12.cloned.1.call-done = bf16[512,768]{1,0:T(8,128)(2,1)} async-done(((bf16[512,768]{1,0:T(8,128)(2,1)}), bf16[512,768]{1,0:T(8,128)(2,1)}) %all-reduce.12.cloned.1.call-update) | async-done | bytes 786448 | tf_op jit(solution)/shard_map/psum | solution.py:211
  240.2 2.8 multiply_reduce_fusion
  243.1 1.4 convert_reduce_fusion.5
  245.0 1.9 multiply_reduce_fusion.5
  247.0 30.7 %while.18 = (s32[]{:T(128)}, f32[512,6,64]{0,2,1:T(8,128)S(1)}, bf16[4,512,384]{2,1,0:T(8,128)(2,1)}, bf16[4,512,384]{2,1,0:T(8,128)(2,1)}, s32[4]{0:T(128)}, /*...) while((s32[]{:T(128)}, f32[512,6,64]{0,2,1:T(8,128)S(1)}, ...), condition=%wide.region_26.27_spmd.clone, body=%wide.region_21.0_spmd.clone.sunk | while | flops 1023939584 | bytes 56297880 | solution.py:272
  247.0 1.3 dynamic_slice.35
  249.0 16.6 %conditional.5 = (f32[512,6,64]{0,2,1:T(8,128)S(1)}, bf16[1,512,384]{1,2,0:T(8,128)(2,1)S(1)}, bf16[1,512,384]{1,2,0:T(8,128)(2,1)S(1)}) conditional(s32[]{:T(128)} %convert_element_type.336, f32[512,6,64]{0,2,1:T(8,128)S(1)} %get-tuple-element.647, (s32[512]{0:T(512)S(1)}, s32[]{:T(128)}, s32[3]{0:T(128)}, s32[]{:T(128)}, ...), branch_computations={%region_22.22_spmd, %region_23.25_spmd} | conditional | flops 1023939584 | bytes 53149304 | solution.py:270
  249.1 4.7 fusion.24
  255.7 5.1 fusion.15
  260.8 1.6 fusion.21
  262.4 1.1 convolution_multiply_fusion.1
  263.5 2.1 fusion.17
  267.1 1.3 dynamic_slice.35
  270.6 1.3 dynamic_slice.35
  274.2 1.3 dynamic_slice.35
  279.1 5.2 fusion.58
  284.3 3.8 fusion.51
  288.2 1.5 fusion.55
  289.7 65.4 %reduce-scatter.3.cloned.1.call-done = bf16[512,384]{1,0:T(8,128)(2,1)} async-done(((bf16[2048,384]{1,0:T(8,128)(2,1)}), bf16[512,384]{1,0:T(8,128)(2,1)}) %reduce-scatter.3.cloned.1.call-update) | async-done | bytes 393232 | tf_op jit(solution)/shard_map/reduce_scatter | solution.py:278
  355.1 1.2 copy.80
  357.9 1.8 fusion.68
  359.7 26.1 %reduce-scatter.5.cloned.1.call-done = bf16[512,384]{1,0:T(8,128)(2,1)} async-done(((bf16[2048,384]{1,0:T(8,128)(2,1)}), bf16[512,384]{1,0:T(8,128)(2,1)}) %reduce-scatter.5.cloned.1.call-update) | async-done | bytes 393232 | tf_op jit(solution)/shard_map/reduce_scatter | solution.py:281
  385.8 3.2 add_convert_fusion.2
  389.1 1.5 convolution_bitcast_fusion.2
  390.6 1.5 convolution_bitcast_fusion.1
  392.1 1.5 convolution_bitcast_fusion
  394.4 61.8 %all-reduce = (f32[384]{0:T(512)}, f32[384]{0:T(512)}, f32[384]{0:T(512)}, f32[768]{0:T(1024)}, f32[768]{0:T(1024)}, /*index=5*/f32[768]{0:T(1024)}, f32[1536]{0...) all-reduce(f32[384]{0:T(512)S(1)} %reduce_sum.234, ...), channel_id=1, replica_groups=mesh['dp'=4,'ctx'=4,'tensor'=2] {'dp','ctx'}, use_global_device_ids=true, to_apply=%region_32.33 | all-reduce | flops 7296 | bytes 58368 | tf_op jit(solution)/shard_map/psum | solution.py:310
  456.2 2.2 add_convert_fusion.1
  458.4 231.9 %all-reduce.16.cloned.1.call-done = (f32[768,384]{0,1:T(8,128)}, f32[768,384]{0,1:T(8,128)}, f32[768,384]{0,1:T(8,128)}, f32[384,768]{1,0:T(8,128)}, f32[768,1536]{1,0:T(8,128)}, /*index=5*/f32[1536,768]{1,0:T(8,128)}) async-done(((f32[768,384]{0,1:T(8,128)}, f32[768,384]{0,1:T(8,128)}, f32[768,384]{0,1:T(8,128)}, f32[384,768]{1,0:T(8,128)}, f32[768,1536]{1,0:T(8,128)}, /*index=5*/f32[1536,768]{1,0:T(8,128)}), ...) | async-done | bytes 14155792 | tf_op jit(solution)/shard_map/psum | solution.py:310
  690.3 2.7 copy.82
  693.1 1.4 copy.83
  694.5 1.4 copy.84
  696.9 5.5 copy.156
  702.4 2.4 copy.157
  (210 shorter events, 27.0 us)
Async XLA Ops:
  7.2 137.0 %copy-start = (bf16[768,1536]{1,0:T(8,128)(2,1)S(1)}, bf16[768,1536]{1,0:T(8,128)(2,1)}, u32[]{:S(2)}) copy-start(bf16[768,1536]{1,0:T(8,128)(2,1)} %param.38) | copy-start | bytes 7077892
  7.2 4.2 copy-start.2
  7.2 4.2 copy-start.52
  7.2 29.1 %all-gather.3.cloned.1.call-start = ((), (), s32[]{:S(2)}) async-start(), calls=%async_computation.2 | async-start | bytes 1966080 | tf_op jit(solution)/shard_map/all_gather | solution.py:151
  8.3 3.1 copy-start.26
  9.5 2.5 copy-start.28
  9.5 2.5 copy-start.30
  12.0 1.9 copy-start.53
  13.8 44.3 %all-gather.5.cloned.1.call-start = ((), (), s32[]{:S(2)}) async-start(), calls=%async_computation.3 | async-start | bytes 1966080 | tf_op jit(solution)/shard_map/all_gather | solution.py:152
  16.3 125.9 %all-reduce.8.cloned.1.call-start = ((), (), s32[]{:S(2)}) async-start(), calls=%async_computation.4 | async-start | bytes 1572864 | tf_op jit(solution)/shard_map/psum | solution.py:183
  60.2 13.1 %copy-start.13 = (pred[512,2048]{1,0:T(8,128)(4,1)}, pred[512,2048]{1,0:T(8,128)(4,1)S(1)}, u32[]{:S(2)}) copy-start(pred[512,2048]{1,0:T(8,128)(4,1)S(1)} %fusion.8) | copy-start | bytes 3145732 | tf_op jit(solution)/shard_map/cond
  104.4 37.8 %copy-start.32 = (f32[768]{0:T(1024)S(1)}, f32[768]{0:T(1024)}, u32[]{:S(2)}) copy-start(f32[768]{0:T(1024)} %param.35) | copy-start | bytes 9220
  107.7 36.5 %copy-start.35 = (f32[768]{0:T(1024)S(1)}, f32[768]{0:T(1024)}, u32[]{:S(2)}) copy-start(f32[768]{0:T(1024)} %param.36) | copy-start | bytes 9220
  107.7 84.8 %all-reduce.10.cloned.1.call-start = ((), (), s32[]{:S(2)}) async-start(), calls=%async_computation.5 | async-start | bytes 1572864 | tf_op jit(solution)/shard_map/psum | solution.py:194
  142.2 1.6 copy-start.10
  142.2 2.0 copy-start.51
  144.2 10.4 %copy-start.36 = (f32[512]{0:T(512)}, f32[512]{0:T(512)S(1)}, u32[]{:S(2)}) copy-start(f32[512]{0:T(512)S(1)} %add_rsqrt_fusion.1) | copy-start | bytes 6148
  144.3 11.5 %copy-start.49 = (bf16[1536,768]{1,0:T(8,128)(2,1)S(1)}, bf16[1536,768]{1,0:T(8,128)(2,1)}, u32[]{:S(2)}) copy-start(bf16[1536,768]{1,0:T(8,128)(2,1)} %param.40) | copy-start | bytes 7077892
  154.6 1.1 copy-start.20
  158.1 82.2 %all-reduce.12.cloned.1.call-start = ((), (), s32[]{:S(2)}) async-start(), calls=%async_computation.6 | async-start | bytes 1572864 | tf_op jit(solution)/shard_map/psum | solution.py:211
  192.5 6.3 copy-start.57
  194.8 1.1 copy-start.18
  194.9 1.1 copy-start.39
  195.2 2.1 copy-start.47
  196.0 2.8 copy-start.56
  197.3 2.0 copy-start.50
  198.8 3.4 copy-start.6
  202.2 1.2 copy-start.54
  205.7 149.3 %reduce-scatter.3.cloned.1.call-start = ((), (), s32[]{:S(2)}) async-start(), calls=%async_computation.7 | async-start | bytes 1966080 | tf_op jit(solution)/shard_map/reduce_scatter | solution.py:278
  210.4 3.2 copy-start.14
  219.1 3.1 copy-start.34
  219.1 21.1 %copy-start.7 = (f32[512,768]{1,0:T(8,128)S(1)}, f32[512,768]{1,0:T(8,128)}, u32[]{:S(2)}) copy-start(f32[512,768]{1,0:T(8,128)} %copy-done.6) | copy-start | bytes 4718596
  219.1 21.1 %copy-start.11 = (bf16[512,768]{1,0:T(8,128)(2,1)S(1)}, bf16[512,768]{1,0:T(8,128)(2,1)}, u32[]{:S(2)}) copy-start(bf16[512,768]{1,0:T(8,128)(2,1)} %all-reduce.8.cloned.1.call-done) | copy-start | bytes 2359300
  240.2 2.9 copy-start.8
  240.2 2.9 copy-start.19
  240.2 2.9 copy-start.37
  243.1 1.4 copy-start.21
  244.5 2.4 copy-start.3
  255.4 8.1 %slice-start = ((s8[6291456]{0:T(1024)(128)(4,1)}), s8[4194304]{0:T(1024)(128)(4,1)S(1)}, s32[]{:S(2)}) async-start(s8[6291456]{0:T(1024)(128)(4,1)} %bitcast.110), calls=%async_computation.11 | async-start | bytes 8388608 | tf_op jit(solution)/shard_map/while/body/eval_jaxpr/cond
  255.6 7.8 %slice-start.1 = ((s8[6291456]{0:T(1024)(128)(4,1)}), s8[2097152]{0:T(1024)(128)(4,1)S(1)}, s32[]{:S(2)}) async-start(s8[6291456]{0:T(1024)(128)(4,1)} %bitcast.110), calls=%async_computation.12 | async-start | bytes 4194304 | tf_op jit(solution)/shard_map/while/body/eval_jaxpr/cond
  277.7 1.4 copy-start.9
  277.7 108.1 %reduce-scatter.5.cloned.1.call-start = ((), (), s32[]{:S(2)}) async-start(), calls=%async_computation.8 | async-start | bytes 1966080 | tf_op jit(solution)/shard_map/reduce_scatter | solution.py:281
  278.5 5.8 copy-start.38
  278.5 5.8 copy-start.48
  278.5 177.7 %all-reduce.14.cloned.1.call-start = ((), (), s32[]{:S(2)}) async-start(), calls=%async_computation.9 | async-start | bytes 1572864 | tf_op jit(solution)/shard_map/psum | solution.py:308
  279.1 5.2 copy-start.12
  279.1 5.2 copy-start.55
  284.3 3.9 copy-start.4
  284.3 3.9 copy-start.17
  288.2 68.0 %copy-start.29 = (f32[512,32]{0,1:T(8,128)S(1)}, f32[512,32]{0,1:T(8,128)}, u32[]{:S(2)}) copy-start(f32[512,32]{0,1:T(8,128)} %copy-done.28) | copy-start | bytes 196612
  288.2 68.1 %copy-start.31 = (f32[512,32]{0,1:T(8,128)S(1)}, f32[512,32]{0,1:T(8,128)}, u32[]{:S(2)}) copy-start(f32[512,32]{0,1:T(8,128)} %copy-done.30) | copy-start | bytes 196612
  356.3 1.1 copy-start.25
  356.7 1.3 copy-start.27
  389.1 301.3 %all-reduce.16.cloned.1.call-start = ((), (), s32[]{:S(2)}) async-start(), calls=%async_computation.10 | async-start | bytes 28311552 | tf_op jit(solution)/shard_map/psum | solution.py:310
  390.6 1.5 copy-start.15
  393.6 0.8 copy-start.45
  393.6 0.8 copy-start.46
  393.6 62.6 %copy-start.5 = (f32[512,768]{1,0:T(8,128)S(1)}, f32[512,768]{1,0:T(8,128)}, u32[]{:S(2)}) copy-start(f32[512,768]{1,0:T(8,128)} %copy-done.3) | copy-start | bytes 4718596
  690.3 2.8 copy-start.24
  693.1 1.4 copy-start.23
  694.5 1.4 copy-start.22
  695.9 6.5 slice-start.2
  696.9 5.5 slice-start.3
  702.4 3.4 copy-start.1
  (7 other events, 5.0 us)
Sparse Core Ops, SparseCore 0:
  13.9 22.3 all-gather.2
  38.4 19.6 all-gather.4
  107.8 34.3 all-reduce.7
  158.2 34.3 all-reduce.9
  205.8 34.3 all-reduce.11
  277.9 77.1 reduce-scatter.2
  357.6 28.1 reduce-scatter.4
  389.2 34.3 all-reduce.13
  429.9 260.4 all-reduce.15
where the time goes:
time: 722 us; the launch traced here: 713 us
  waiting for transfers between devices  450 us (62%)
  matrix products  86 us (12%)
  blocking collectives  61.8 us (9%)
  local copies, waits for them, and re-layouts  53.3 us (7%)
  other arithmetic  42.3 us (6%)
  between operations  14.8 us (2%)
    psum x1, waiting for transfers between devices, per_device(): lax.psum((query_weight_grad, query_bias_grad, key_weight_grad, key_bias_g...  232 us
    reduce_scatter x1, waiting for transfers between devices, per_device(): lax.psum_scatter(key_terms.astype(jnp.bfloat16), 'ctx', scatter_dimension...  65.4 us
    psum x1, blocking collectives, per_device(): lax.psum((query_weight_grad, query_bias_grad, key_weight_grad, key_bias_g...  61.8 us
    psum x1, waiting for transfers between devices, per_device(): lax.psum(matmul(hidden, outer_weight).astype(jnp.bfloat16), 'tensor')  34.4 us
    psum x1, waiting for transfers between devices, per_device(): lax.psum(matmul(attended_low, output_weight).astype(jnp.bfloat16), 'tensor')  34.2 us
    unnamed x126, local copies, waits for them, and re-layouts  28.1 us
    reduce_scatter x1, waiting for transfers between devices, per_device(): lax.psum_scatter(value_terms.astype(jnp.bfloat16), 'ctx', scatter_dimensi...  26.1 us
    all_gather x1, waiting for transfers between devices, per_device(): lax.all_gather(value_flat, 'ctx', axis=0, tiled=True)  21.8 us
  transfers between devices with their start and end apart: 9, of which 8 were waited for; matrix products, arithmetic and copies ran while one was open for 6% of the time, Pallas kernels for 0%

commit v1 on v0

v1 whole, which is shorter than its diff:
```python
import functools

import jax
import jax.numpy as jnp
import numpy as np
from jax import lax
from jax.experimental import pallas as pl
from jax.experimental.pallas import tpu as pltpu
from jax.sharding import PartitionSpec as P

HEAD_DIM = 64
PAIR = 2 * HEAD_DIM
MASKED = -1e30
EPSILON = 1e-06
TILE = 256
F32 = jnp.float32
BF16 = jnp.bfloat16
VMEM_BYTES = 56 * 1024 * 1024

NN = (((1,), (0,)), ((), ()))
NT = (((1,), (1,)), ((), ()))
TN = (((0,), (0,)), ((), ()))


def dot(left, right, dims=NN):
    return lax.dot_general(left, right, dims, preferred_element_type=F32)


def call(kernel, grid, in_specs, out_specs, out_shape, scratch=(), flops=0, bytes_accessed=0, scalars=0):
    return pl.pallas_call(
        kernel,
        grid_spec=pltpu.PrefetchScalarGridSpec(
            num_scalar_prefetch=scalars,
            grid=grid,
            in_specs=in_specs,
            out_specs=out_specs,
            scratch_shapes=scratch,
        ),
        out_shape=out_shape,
        compiler_params=pltpu.CompilerParams(vmem_limit_bytes=VMEM_BYTES),
        cost_estimate=pl.CostEstimate(
            flops=int(flops), bytes_accessed=int(bytes_accessed), transcendentals=0
        ),
    )


def whole(shape):
    return pl.BlockSpec(shape, lambda *_: (0,) * len(shape))


def columns(rows, width, scale=1, shift=0):
    return pl.BlockSpec((rows, width), lambda p, *_: (0, scale * p + shift))


def rowblock(height, width):
    return pl.BlockSpec((height, width), lambda p, *_: (p, 0))


def swap_halves(value):
    lane = lax.broadcasted_iota(jnp.int32, value.shape, 1)
    ahead = pltpu.roll(value, PAIR - HEAD_DIM // 2, 1)
    behind = pltpu.roll(value, HEAD_DIM // 2, 1)
    return jnp.where(lane % HEAD_DIM < HEAD_DIM // 2, ahead, behind)


def project_kernel(
    info, tokens, wq, wk, wv, bias, base_cos, base_sin, freq, q_out, kv_out, cos_out, sin_out
):
    rows = tokens.shape[0]

    @pl.when(pl.program_id(0) == 0)
    def _():
        offset, end0, end1 = info[0], info[1], info[2]
        row = offset + lax.broadcasted_iota(jnp.int32, (rows, 1), 0)
        turns = []
        for start in (0, end0, end1):
            angle = (offset - start).astype(F32) * freq[...]
            turns.append((jnp.cos(angle), jnp.sin(angle)))
        late, later = row >= end0, row >= end1
        cos_turn = jnp.where(later, turns[2][0], jnp.where(late, turns[1][0], turns[0][0]))
        sin_turn = jnp.where(later, turns[2][1], jnp.where(late, turns[1][1], turns[0][1]))
        cosine = base_cos[...] * cos_turn - base_sin[...] * sin_turn
        sine = base_sin[...] * cos_turn + base_cos[...] * sin_turn
        lane = lax.broadcasted_iota(jnp.int32, (rows, PAIR), 1)
        cos_out[...] = cosine
        sin_out[...] = jnp.where(lane % HEAD_DIM < HEAD_DIM // 2, -sine, sine)

    weight = jnp.concatenate([wq[...], wk[...], wv[...]], axis=1)
    pre = dot(tokens[...], weight)
    cosine, sine = cos_out[...], sin_out[...]
    query = pre[:, :PAIR] + bias[0:1, :]
    key = pre[:, PAIR : 2 * PAIR] + bias[1:2, :]
    q_out[...] = (query * cosine + swap_halves(query) * sine).astype(BF16)
    kv_out[:, :PAIR] = (key * cosine + swap_halves(key) * sine).astype(BF16)
    kv_out[:, PAIR:] = (pre[:, 2 * PAIR :] + bias[2:3, :]).astype(BF16)


def start_of(index, end0, end1):
    return jnp.where(index >= end1, end1, jnp.where(index >= end0, end0, 0))


def needed(info, query_row, key_row):
    end0, end1, span = info[1], info[2], info[3]
    return (
        (key_row <= query_row + TILE - 1)
        & (key_row + TILE - 1 >= start_of(query_row, end0, end1))
        & (query_row < span)
        & (key_row >= 0)
    )


def allowed(info, query_row, key_row):
    query = query_row + lax.broadcasted_iota(jnp.int32, (1, TILE), 1)
    key = key_row + lax.broadcasted_iota(jnp.int32, (TILE, 1), 0)
    return (key >= start_of(query, info[1], info[2])) & (key <= query)


def head_mask(shape, head):
    lane = lax.broadcasted_iota(jnp.int32, shape, 1)
    return (lane // HEAD_DIM) == head


def tile(index):
    return pl.ds(pl.multiple_of(index * TILE, TILE), TILE)


def attend_kernel(
    info, q, kv_own, kv_mate, kv_far, kv_cross, wo,
    low_out, high_out, lse_out, part_out, q_masked, peak, total, accum, attn_sum,
):
    rows = q.shape[0]
    tiles = rows // TILE
    offset = info[0]
    step = pl.program_id(0)
    for head in range(2):
        q_masked[head] = jnp.where(head_mask(q.shape, head), q[...] * 0.125, 0).astype(BF16)

    def visit(kv, query_tile, key_tile, query_row, key_row, first):
        mask = allowed(info, query_row, key_row)
        keys = kv[tile(key_tile), :PAIR]
        values = kv[tile(key_tile), PAIR:]
        for head in range(2):
            lanes = tile(query_tile)
            scores = dot(keys, q_masked[head, tile(query_tile), :], NT)
            scores = jnp.where(mask, scores, MASKED)
            top = jnp.max(scores, axis=0, keepdims=True)
            if first:
                prob = jnp.exp(scores - top)
                total[head : head + 1, lanes] = jnp.sum(prob, axis=0, keepdims=True)
                accum[head, :, lanes] = dot(values, prob.astype(BF16), TN)
                peak[head : head + 1, lanes] = top
            else:
                old = peak[head : head + 1, lanes]
                top = jnp.maximum(old, top)
                decay = jnp.exp(old - top)
                prob = jnp.exp(scores - top)
                total[head : head + 1, lanes] = total[
                    head : head + 1, lanes
                ] * decay + jnp.sum(prob, axis=0, keepdims=True)
                accum[head, :, lanes] = accum[head, :, lanes] * decay + dot(
                    values, prob.astype(BF16), TN
                )
                peak[head : head + 1, lanes] = top

    for query_tile in range(tiles):
        query_row = offset + query_tile * TILE
        visit(kv_own, query_tile, query_tile, query_row, query_row, True)
        for key_tile in range(query_tile):
            key_row = offset + key_tile * TILE

            @pl.when(needed(info, query_row, key_row))
            def _():
                visit(kv_own, query_tile, key_tile, query_row, key_row, False)

    for slot, kv in enumerate((kv_mate, kv_far, kv_cross)):
        for query_tile in range(tiles):
            for key_tile in range(tiles):
                query_row = offset + query_tile * TILE
                key_row = info[4 + slot] * rows + key_tile * TILE

                @pl.when((info[4 + slot] < info[0] // rows) & needed(info, query_row, key_row))
                def _():
                    visit(kv, query_tile, key_tile, query_row, key_row, False)

    for head in range(2):
        sums = total[head : head + 1, :]
        lse_out[0, head : head + 1, :] = peak[head : head + 1, :] + jnp.log(sums)
        high_out[HEAD_DIM * head : HEAD_DIM * (head + 1), :] = accum[
            head, HEAD_DIM * head : HEAD_DIM * (head + 1), :
        ] / sums
    low = high_out[...].T.astype(BF16)
    low_out[...] = low
    part = dot(low, wo[...])

    @pl.when(step == 0)
    def _():
        attn_sum[...] = part

    @pl.when(step > 0)
    def _():
        attn_sum[...] += part

    @pl.when(step == pl.num_programs(0) - 1)
    def _():
        part_out[...] = attn_sum[...].astype(BF16)


def mean(value):
    return jnp.mean(value, axis=-1, keepdims=True)


def normalize(rows_in):
    centered = rows_in - mean(rows_in)
    inverse = lax.rsqrt(mean(centered * centered) + EPSILON)
    return centered * inverse, inverse


def norm_back(grad, normed, inverse):
    return inverse * (grad - mean(grad) - normed * mean(grad * normed))


def forward_kernel(
    tokens, part, other, vectors, w_in, b_in, w_out,
    normed_out, inverse_out, first_out, hidden_out, slope_out, part_out, accum,
):
    step = pl.program_id(0)

    @pl.when(step == 0)
    def _():
        attn = part[...].astype(F32) + other[...].astype(F32) + vectors[0:1, :]
        normed, inverse = normalize(tokens[...].astype(F32) + attn)
        normed_out[...] = normed
        inverse_out[...] = inverse
        first_out[...] = (normed * vectors[1:2, :] + vectors[2:3, :]).astype(BF16)

    pre = dot(first_out[...], w_in[...]) + b_in[...]
    cdf = 0.5 * (1.0 + lax.erf(pre * 0.7071067811865476))
    hidden = (pre * cdf).astype(BF16)
    hidden_out[...] = hidden
    slope_out[...] = (cdf + pre * (jnp.exp(-0.5 * pre * pre) * 0.3989422804014327)).astype(BF16)
    product = dot(hidden, w_out[...])

    @pl.when(step == 0)
    def _():
        accum[...] = product

    @pl.when(step > 0)
    def _():
        accum[...] += product

    @pl.when(step == pl.num_programs(0) - 1)
    def _():
        part_out[...] = accum[...].astype(BF16)


def backward_kernel(
    normed_first, part, other, out_grad, vectors, slope, w_in, w_out,
    layer_out, ffn_grad_out, pre_grad_out, part_out, res_out, sums_out, inner_out, accum,
):
    step = pl.program_id(0)

    @pl.when(step == 0)
    def _():
        first = normed_first[...] * vectors[1:2, :] + vectors[2:3, :]
        ffn = part[...].astype(F32) + other[...].astype(F32) + vectors[3:4, :]
        normed, inverse = normalize(first + ffn)
        layer_out[...] = (normed * vectors[4:5, :] + vectors[5:6, :]).astype(BF16)
        upstream = out_grad[...].astype(F32)
        res_grad = norm_back(upstream * vectors[4:5, :], normed, inverse)
        ffn_grad = res_grad.astype(BF16)
        res_out[...] = res_grad
        ffn_grad_out[...] = ffn_grad
        sums_out[...] = jnp.zeros_like(sums_out)
        sums_out[0:1, :] = jnp.sum(upstream * normed, axis=0, keepdims=True)
        sums_out[1:2, :] = jnp.sum(upstream, axis=0, keepdims=True)
        sums_out[2:3, :] = jnp.sum(ffn_grad.astype(F32), axis=0, keepdims=True)

    hidden_grad = dot(ffn_grad_out[...], w_out[...], NT)
    pre_grad = (hidden_grad * slope[...].astype(F32)).astype(BF16)
    pre_grad_out[...] = pre_grad
    inner_out[...] = jnp.sum(pre_grad.astype(F32), axis=0, keepdims=True)
    product = dot(pre_grad, w_in[...], NT)

    @pl.when(step == 0)
    def _():
        accum[...] = product

    @pl.when(step > 0)
    def _():
        accum[...] += product

    @pl.when(step == pl.num_programs(0) - 1)
    def _():
        part_out[...] = accum[...].astype(BF16)


def middle_kernel(
    res_second, part, other, normed, inverse, vectors, wo, high,
    res_out, grad_out, head_out, dot_out, sums_out,
):
    first_grad = res_second[...] + part[...].astype(F32) + other[...].astype(F32)
    unit = normed[...]
    res_grad = norm_back(first_grad * vectors[1:2, :], unit, inverse[...])
    attn_grad = res_grad.astype(BF16)
    res_out[...] = res_grad
    grad_out[...] = attn_grad
    sums_out[...] = jnp.zeros_like(sums_out)
    sums_out[0:1, :] = jnp.sum(first_grad * unit, axis=0, keepdims=True)
    sums_out[1:2, :] = jnp.sum(first_grad, axis=0, keepdims=True)
    sums_out[2:3, :] = jnp.sum(attn_grad.astype(F32), axis=0, keepdims=True)
    head_out[...] = dot(attn_grad, wo[...], NT).astype(BF16)
    turned = dot(wo[...], attn_grad, NT).astype(BF16).astype(F32) * high[...]
    for head in range(wo.shape[0] // HEAD_DIM):
        dot_out[head // 2, head % 2, :] = jnp.sum(
            turned[HEAD_DIM * head : HEAD_DIM * (head + 1), :], axis=0
        )


def attend_back_kernel(
    info, q, grad, kv_own, lse, rowdot, kv_mate, kv_far, kv_cross,
    q_mate, q_far, q_cross, grad_mate, grad_far, grad_cross,
    lse_mate, lse_far, lse_cross, rowdot_mate, rowdot_far, rowdot_cross,
    tokens, wq, wk, wv, cosine, sine,
    q_grad_out, k_grad_out, v_grad_out, bias_out, part_out,
    q_masked, grad_masked, k_masked, v_masked, q_turned, k_turned, v_sum, tokens_turned, accum,
):
    rows = q.shape[0]
    tiles = rows // TILE
    offset = info[0]
    me = offset // rows
    step = pl.program_id(0)

    @pl.when(step == 0)
    def _():
        tokens_turned[...] = tokens[...].T

    for head in range(2):
        mask = head_mask(q.shape, head)
        q_masked[head] = jnp.where(mask, q[...] * 0.125, 0).astype(BF16)
        grad_masked[head] = jnp.where(mask, grad[...], 0).astype(BF16)
        k_masked[head] = jnp.where(mask, kv_own[:, :PAIR] * 0.125, 0).astype(BF16)
        v_masked[head] = jnp.where(mask, kv_own[:, PAIR:], 0).astype(BF16)
    q_turned[...] = jnp.zeros_like(q_turned)
    k_turned[...] = jnp.zeros_like(k_turned)
    v_sum[...] = jnp.zeros_like(v_sum)

    def pair_terms(keys, values, queries, grads, mask, log_row, dot_row):
        scores = jnp.where(mask, dot(keys, queries, NT), MASKED)
        prob = jnp.exp(scores - log_row)
        prob_grad = dot(values, grads, NT)
        return prob.astype(BF16), (prob * (prob_grad - dot_row)).astype(BF16)

    def visit_queries(kv, query_tile, key_tile, query_row, key_row, own):
        mask = allowed(info, query_row, key_row)
        lanes = tile(query_tile)
        keys = kv[tile(key_tile), :PAIR]
        values = kv[tile(key_tile), PAIR:]
        for head in range(2):
            prob, score_grad = pair_terms(
                keys, values, q_masked[head, lanes, :], grad_masked[head, lanes, :], mask,
                lse[0, head : head + 1, lanes], rowdot[0, head : head + 1, lanes],
            )
            span = slice(HEAD_DIM * head, HEAD_DIM * (head + 1))
            q_turned[span, lanes] += dot(keys, score_grad, TN)[span, :]
            if own:
                k_turned[head, tile(key_tile), :] += dot(score_grad, q[lanes, :])
                v_sum[head, tile(key_tile), :] += dot(prob, grad[lanes, :])

    def visit_keys(queries, grads, logs, dots, query_tile, key_tile, query_row, key_row):
        mask = allowed(info, query_row, key_row)
        lanes = tile(query_tile)
        for head in range(2):
            prob, score_grad = pair_terms(
                k_masked[head, tile(key_tile), :], v_masked[head, tile(key_tile), :],
                queries[lanes, :], grads[lanes, :], mask,
                logs[0, head : head + 1, lanes], dots[0, head : head + 1, lanes],
            )
            k_turned[head, tile(key_tile), :] += dot(score_grad, queries[lanes, :])
            v_sum[head, tile(key_tile), :] += dot(prob, grads[lanes, :])

    for query_tile in range(tiles):
        for key_tile in range(query_tile + 1):
            query_row = offset + query_tile * TILE
            key_row = offset + key_tile * TILE

            @pl.when(needed(info, query_row, key_row))
            def _():
                visit_queries(kv_own, query_tile, key_tile, query_row, key_row, True)

    for slot, kv in enumerate((kv_mate, kv_far, kv_cross)):
        for query_tile in range(tiles):
            for key_tile in range(tiles):
                query_row = offset + query_tile * TILE
                key_row = info[4 + slot] * rows + key_tile * TILE

                @pl.when((info[4 + slot] < me) & needed(info, query_row, key_row))
                def _():
                    visit_queries(kv, query_tile, key_tile, query_row, key_row, False)

    later = (
        (q_mate, grad_mate, lse_mate, rowdot_mate),
        (q_far, grad_far, lse_far, rowdot_far),
        (q_cross, grad_cross, lse_cross, rowdot_cross),
    )
    for slot, (queries, grads, logs, dots) in enumerate(later):
        for key_tile in range(tiles):
            for query_tile in range(tiles):
                query_row = info[7 + slot] * rows + query_tile * TILE
                key_row = offset + key_tile * TILE

                @pl.when((info[7 + slot] > me) & needed(info, query_row, key_row))
                def _():
                    visit_keys(
                        queries, grads, logs, dots, query_tile, key_tile, query_row, key_row
                    )

    first_head = head_mask(q.shape, 0)
    cosines, sines = cosine[...], sine[...]

    def turn_back(value):
        return (value * cosines - swap_halves(value) * sines).astype(BF16)

    q_grad = turn_back(q_turned[...].T * 0.125)
    k_grad = turn_back(jnp.where(first_head, k_turned[0], k_turned[1]) * 0.125)
    v_grad = jnp.where(first_head, v_sum[0], v_sum[1]).astype(BF16)
    bias_out[...] = jnp.zeros_like(bias_out)
    for index, value in enumerate((q_grad, k_grad, v_grad)):
        bias_out[index : index + 1, :] = jnp.sum(value.astype(F32), axis=0, keepdims=True)
    together = jnp.concatenate([q_grad, k_grad, v_grad], axis=1)
    weight_grad = dot(tokens_turned[...], together).astype(BF16)
    q_grad_out[...] = weight_grad[:, :PAIR]
    k_grad_out[...] = weight_grad[:, PAIR : 2 * PAIR]
    v_grad_out[...] = weight_grad[:, 2 * PAIR :]
    weights = jnp.concatenate([wq[...], wk[...], wv[...]], axis=1)
    part = dot(together, weights, NT)

    @pl.when(step == 0)
    def _():
        accum[...] = part

    @pl.when(step > 0)
    def _():
        accum[...] += part

    @pl.when(step == pl.num_programs(0) - 1)
    def _():
        part_out[...] = accum[...].astype(BF16)


def left_contract(left_side, right_side):
    return jnp.einsum("ti,tj->ij", left_side, right_side, preferred_element_type=F32)


def exchange_stages(ctx_size, dp_size):
    def bits(axis, size):
        return [(axis, 1 << i) for i in range((size - 1).bit_length())]

    ctx, dp = bits("ctx", ctx_size), bits("dp", dp_size)
    return ctx[:1] + ctx[1:] + dp, ctx[:1] + dp + ctx[1:]


def flip(value, axis, bit):
    size = lax.axis_size(axis)
    return lax.ppermute(value, axis, [(i, i ^ bit) for i in range(size)])


def set_bit(axis, bit):
    return (lax.axis_index(axis) & bit) != 0


def sum_everywhere(value, stages):
    for axis, bit in stages:
        half = value.shape[0] // 2
        upper = set_bit(axis, bit).astype(jnp.int32)
        send = lax.dynamic_slice_in_dim(value, (1 - upper) * half, half, 0)
        keep = lax.dynamic_slice_in_dim(value, upper * half, half, 0)
        received = flip(send, axis, bit)
        value = (keep.astype(F32) + received.astype(F32)).astype(value.dtype)
    for axis, bit in reversed(stages):
        received = flip(value, axis, bit)
        upper = set_bit(axis, bit)
        value = jnp.where(
            upper,
            jnp.concatenate([received, value], axis=0),
            jnp.concatenate([value, received], axis=0),
        )
    return value


def per_device(
    tokens, out_grad, lengths, query_weight, query_bias, key_weight, key_bias, value_weight,
    value_bias, output_weight, output_bias, first_gain, first_shift, inner_weight, inner_bias,
    outer_weight, outer_bias, second_gain, second_shift,
):
    rows, width = tokens.shape
    local = query_weight.shape[1]
    pairs = local // PAIR
    hidden_width = inner_weight.shape[1]
    ctx_size, dp_size = lax.axis_size("ctx"), lax.axis_size("dp")
    me = lax.axis_index("ctx")
    mate = me ^ 1
    info = jnp.stack(
        [
            me * rows, lengths[0, 0], lengths[0, 0] + lengths[0, 1],
            jnp.int32(ctx_size * rows), mate, me - 2, mate - 2, mate, me + 2, mate + 2,
        ]
    ).astype(jnp.int32)

    frequency = 10000.0 ** (-2.0 * np.arange(HEAD_DIM // 2) / HEAD_DIM)
    lanes = np.tile(frequency, PAIR // (HEAD_DIM // 2))
    angles = np.arange(rows)[:, None] * lanes[None, :]
    base_cos = jnp.asarray(np.cos(angles), F32)
    base_sin = jnp.asarray(np.sin(angles), F32)
    bias = jnp.stack([query_bias, key_bias, value_bias])

    def shape(*dims, dtype=BF16):
        return jax.ShapeDtypeStruct(dims, dtype)

    queries, kv_own, cosine, sine = call(
        project_kernel,
        (pairs,),
        [
            whole((rows, width)), columns(width, PAIR), columns(width, PAIR), columns(width, PAIR),
            columns(3, PAIR), whole((rows, PAIR)), whole((rows, PAIR)), whole((1, PAIR)),
        ],
        [
            columns(rows, PAIR), columns(rows, 2 * PAIR), whole((rows, PAIR)), whole((rows, PAIR)),
        ],
        [
            shape(rows, local), shape(rows, 2 * local),
            shape(rows, PAIR, dtype=F32), shape(rows, PAIR, dtype=F32),
        ],
        flops=6 * rows * width * local,
        bytes_accessed=2 * (rows * width + 3 * width * local + 3 * rows * local),
        scalars=1,
    )(
        info, tokens, query_weight, key_weight, value_weight, bias, base_cos, base_sin,
        jnp.asarray(lanes[None, :], F32),
    )

    forward_pairs = [(i, i + 2) for i in range(ctx_size - 2)]
    backward_pairs = [(i + 2, i) for i in range(ctx_size - 2)]

    def spread(value, pairs_list):
        far = lax.ppermute(value, "ctx", pairs_list)
        return flip(value, "ctx", 1), far, flip(far, "ctx", 1)

    kv_mate, kv_far, kv_cross = spread(kv_own, forward_pairs)

    stat = pl.BlockSpec((1, 2, rows), lambda p, *_: (p, 0, 0))
    kv_spec = columns(rows, 2 * PAIR)
    pair_spec = columns(rows, PAIR)
    low, high, lse, attn_part = call(
        attend_kernel,
        (pairs,),
        [pair_spec, kv_spec, kv_spec, kv_spec, kv_spec, rowblock(PAIR, width)],
        [pair_spec, rowblock(PAIR, rows), stat, whole((rows, width))],
        [
            shape(rows, local), shape(local, rows, dtype=F32),
            shape(pairs, 2, rows, dtype=F32), shape(rows, width),
        ],
        scratch=[
            pltpu.VMEM((2, rows, PAIR), BF16), pltpu.VMEM((2, rows), F32),
            pltpu.VMEM((2, rows), F32), pltpu.VMEM((2, PAIR, rows), F32),
            pltpu.VMEM((rows, width), F32),
        ],
        flops=4 * rows * 2 * rows * local,
        bytes_accessed=12 * rows * local,
        scalars=1,
    )(info, queries, kv_own, kv_mate, kv_far, kv_cross, output_weight)

    q_mate, q_far, q_cross = spread(queries, backward_pairs)
    lse_mate, lse_far, lse_cross = spread(lse, backward_pairs)

    def swap(value):
        return flip(value, "tensor", 1)

    vectors = jnp.stack(
        [output_bias, first_gain, first_shift, outer_bias, second_gain, second_shift]
    )
    unit = hidden_width // 3
    row_spec = whole((rows, width))
    vec_spec = whole((6, width))
    attn_other = swap(attn_part)
    normed_first, inverse_first, first_low, hidden, slope, ffn_part = call(
        forward_kernel,
        (3,),
        [
            row_spec, row_spec, row_spec, vec_spec, columns(width, unit), columns(1, unit),
            rowblock(unit, width),
        ],
        [
            row_spec, whole((rows, 1)), row_spec, columns(rows, unit), columns(rows, unit),
            row_spec,
        ],
        [
            shape(rows, width, dtype=F32), shape(rows, 1, dtype=F32), shape(rows, width),
            shape(rows, hidden_width), shape(rows, hidden_width), shape(rows, width),
        ],
        scratch=[pltpu.VMEM((rows, width), F32)],
        flops=4 * rows * width * hidden_width,
        bytes_accessed=4 * width * hidden_width + 8 * rows * hidden_width,
    )(
        tokens, attn_part, attn_other, vectors, inner_weight, inner_bias[None, :], outer_weight
    )

    ffn_other = swap(ffn_part)
    layer_out, ffn_grad, pre_grad, first_part, res_second, second_sums, inner_sums = call(
        backward_kernel,
        (3,),
        [
            row_spec, row_spec, row_spec, row_spec, vec_spec, columns(rows, unit),
            columns(width, unit), rowblock(unit, width),
        ],
        [
            row_spec, row_spec, columns(rows, unit), row_spec, row_spec, whole((8, width)),
            columns(1, unit),
        ],
        [
            shape(rows, width), shape(rows, width), shape(rows, hidden_width),
            shape(rows, width), shape(rows, width, dtype=F32), shape(8, width, dtype=F32),
            shape(1, hidden_width, dtype=F32),
        ],
        scratch=[pltpu.VMEM((rows, width), F32)],
        flops=4 * rows * width * hidden_width,
        bytes_accessed=4 * width * hidden_width + 8 * rows * hidden_width,
    )(
        normed_first, ffn_part, ffn_other, out_grad, vectors, slope, inner_weight, outer_weight
    )

    first_other = swap(first_part)
    x_first, z_first = exchange_stages(ctx_size, dp_size)
    outer_weight_grad = sum_everywhere(left_contract(hidden, ffn_grad).astype(BF16), x_first)
    inner_weight_grad = sum_everywhere(left_contract(first_low, pre_grad).astype(BF16), z_first)

    res_first, attn_grad, head_grad, rowdot, first_sums = call(
        middle_kernel,
        (1,),
        [
            row_spec, row_spec, row_spec, row_spec, whole((rows, 1)), vec_spec,
            whole((local, width)), whole((local, rows)),
        ],
        [
            row_spec, row_spec, whole((rows, local)), whole((pairs, 2, rows)), whole((8, width)),
        ],
        [
            shape(rows, width, dtype=F32), shape(rows, width), shape(rows, local),
            shape(pairs, 2, rows, dtype=F32), shape(8, width, dtype=F32),
        ],
        flops=4 * rows * width * local,
        bytes_accessed=20 * rows * width,
    )(
        res_second, first_part, first_other, normed_first, inverse_first, vectors,
        output_weight, high,
    )

    grad_mate, grad_far, grad_cross = spread(head_grad, backward_pairs)
    rowdot_mate, rowdot_far, rowdot_cross = spread(rowdot, backward_pairs)

    q_weight_grad, k_weight_grad, v_weight_grad, bias_sums, input_part = call(
        attend_back_kernel,
        (pairs,),
        [pair_spec, pair_spec, kv_spec, stat, stat]
        + [kv_spec] * 3
        + [pair_spec] * 6
        + [stat] * 6
        + [whole((rows, width))]
        + [columns(width, PAIR)] * 3
        + [whole((rows, PAIR))] * 2,
        [columns(width, PAIR)] * 3 + [columns(8, PAIR), whole((rows, width))],
        [shape(width, local)] * 3 + [shape(8, local, dtype=F32), shape(rows, width)],
        scratch=[
            pltpu.VMEM((2, rows, PAIR), BF16), pltpu.VMEM((2, rows, PAIR), BF16),
            pltpu.VMEM((2, rows, PAIR), BF16), pltpu.VMEM((2, rows, PAIR), BF16),
            pltpu.VMEM((PAIR, rows), F32), pltpu.VMEM((2, rows, PAIR), F32),
            pltpu.VMEM((2, rows, PAIR), F32), pltpu.VMEM((width, rows), BF16),
            pltpu.VMEM((rows, width), F32),
        ],
        flops=10 * rows * 2 * rows * local,
        bytes_accessed=40 * rows * local,
        scalars=1,
    )(
        info, queries, head_grad, kv_own, lse, rowdot, kv_mate, kv_far, kv_cross,
        q_mate, q_far, q_cross, grad_mate, grad_far, grad_cross,
        lse_mate, lse_far, lse_cross, rowdot_mate, rowdot_far, rowdot_cross,
        tokens, query_weight, key_weight, value_weight, cosine, sine,
    )

    input_other = swap(input_part)
    output_weight_grad = sum_everywhere(left_contract(low, attn_grad).astype(BF16), x_first)
    qk_weight_grad = sum_everywhere(
        jnp.concatenate([q_weight_grad, k_weight_grad], axis=1), x_first
    )
    v_weight_grad = sum_everywhere(v_weight_grad, z_first)
    input_grad = (res_first + input_part.astype(F32) + input_other.astype(F32)).astype(BF16)

    packed = jnp.concatenate(
        [
            second_sums[:3], first_sums[:3], inner_sums.reshape(-1, width),
            jnp.pad(bias_sums[:3], ((0, 0), (0, width - local))),
        ],
        axis=0,
    )
    packed = jnp.pad(packed, ((0, -packed.shape[0] % 16), (0, 0)))
    for axis, bit in x_first:
        packed = packed + flip(packed, axis, bit)
    inner_rows = hidden_width // width
    last = 6 + inner_rows
    return (
        layer_out,
        input_grad,
        qk_weight_grad[:, :local].astype(F32),
        packed[last, :local],
        qk_weight_grad[:, local:].astype(F32),
        packed[last + 1, :local],
        v_weight_grad.astype(F32),
        packed[last + 2, :local],
        output_weight_grad.astype(F32),
        packed[5],
        packed[3],
        packed[4],
        inner_weight_grad.astype(F32),
        packed[6 : 6 + inner_rows].reshape(-1),
        outer_weight_grad.astype(F32),
        packed[2],
        packed[0],
        packed[1],
    )


def solution(mesh):
    rows_spec, column_spec, row_spec = P(("dp", "ctx"), None), P(None, "tensor"), P("tensor", None)
    return jax.shard_map(
        per_device,
        mesh=mesh,
        in_specs=(
            rows_spec, rows_spec, P("dp", None),
            column_spec, P("tensor"), column_spec, P("tensor"), column_spec, P("tensor"),
            row_spec, P(), P(), P(), column_spec, P("tensor"), row_spec, P(), P(), P(),
        ),
        out_specs=(
            rows_spec, rows_spec,
            column_spec, P("tensor"), column_spec, P("tensor"), column_spec, P("tensor"),
            row_spec, P(), P(), P(), column_spec, P("tensor"), row_spec, P(), P(), P(),
        ),
        check_vma=False,
    )
```

time: 722 us -> 351 us (0.49)
  waiting for transfers between devices: 450 us -> 122 us
  starting transfers between devices: 1.01 us -> 96 us
  matrix products: 86 us -> 4.62 us
  Pallas kernels: 0 us -> 80.1 us
  blocking collectives: 61.8 us -> 0 us
  local copies, waits for them, and re-layouts: 53.3 us -> 19.1 us
  other arithmetic: 42.3 us -> 23.5 us
  between operations: 14.8 us -> 3.13 us
    psum x5 -> x0, waiting for transfers between devices: 317 us -> none  [the longest x1 232 us: per_device(): lax.psum((query_weight_grad, query_bias_grad, key_weight_grad, key_bias_g...]
    ppermute x0 -> x63, waiting for transfers between devices: none -> 122 us  [the longest x58 87.7 us: flip(): return lax.ppermute(value, axis, [(i, i ^ bit) for i in range(size)])]
    ppermute x0 -> x63, starting transfers between devices: none -> 96 us  [the longest x58 86 us: flip(): return lax.ppermute(value, axis, [(i, i ^ bit) for i in range(size)])]
    reduce_scatter x2 -> x0, waiting for transfers between devices: 91.5 us -> none  [the longest x1 65.4 us: per_device(): lax.psum_scatter(key_terms.astype(jnp.bfloat16), 'ctx', scatter_dimension...]
    dot_general x25 -> x3, matrix products: 86 us -> 4.62 us  [left_contract(): jnp.einsum('ti,tj->ij', left_side, right_side, preferred_element_type=F32)]
    pallas_call x0 -> x6, Pallas kernels: none -> 80.1 us  [the longest x1 35.2 us: per_device(): call(attend_back_kernel, (pairs,), [pair_spec, pair_spec, kv_spec, stat,...]
    psum x1 -> x0, blocking collectives: 61.8 us -> none  [per_device(): lax.psum((query_weight_grad, query_bias_grad, key_weight_grad, key_bias_g...]
    all_gather x2 -> x0, waiting for transfers between devices: 40.8 us -> none  [the longest x1 21.8 us: per_device(): lax.all_gather(value_flat, 'ctx', axis=0, tiled=True)]
  transfers between devices with their start and end apart: 9 -> 63, of which waited for: 8 -> 30; matrix products, arithmetic and copies ran while one was open for 6% -> 10% of each run, Pallas kernels for 0% -> 12%
where the time goes in v1:
time: 351 us; the launch traced here: 348 us
  waiting for transfers between devices  122 us (35%)
  starting transfers between devices  96 us (27%)
  Pallas kernels  80.1 us (23%)
  other arithmetic  23.5 us (7%)
  local copies, waits for them, and re-layouts  19.1 us (5%)
  matrix products  4.62 us (1%)
    ppermute x58, waiting for transfers between devices, flip(): return lax.ppermute(value, axis, [(i, i ^ bit) for i in range(size)])  87.7 us
    ppermute x58, starting transfers between devices, flip(): return lax.ppermute(value, axis, [(i, i ^ bit) for i in range(size)])  86 us
    pallas_call x1, Pallas kernels, per_device(): call(attend_back_kernel, (pairs,), [pair_spec, pair_spec, kv_spec, stat,...  35.2 us
    ppermute x5, waiting for transfers between devices, spread(): far = lax.ppermute(value, 'ctx', pairs_list)  34 us
    pallas_call x1, Pallas kernels, per_device(): call(attend_kernel, (pairs,), [pair_spec, kv_spec, kv_spec, kv_spec, kv_s...  11.9 us
    pallas_call x1, Pallas kernels, per_device(): call(backward_kernel, (3,), [row_spec, row_spec, row_spec, row_spec, vec_...  11.5 us
    ppermute x5, starting transfers between devices, spread(): far = lax.ppermute(value, 'ctx', pairs_list)  10 us
    pallas_call x1, Pallas kernels, per_device(): call(forward_kernel, (3,), [row_spec, row_spec, row_spec, vec_spec, colum...  9.67 us
  transfers between devices with their start and end apart: 63, of which 30 were waited for; matrix products, arithmetic and copies ran while one was open for 10% of the time, Pallas kernels for 12%

profile of v1, /device:TPU:0, one launch (start us, length us, event | category | flops | bytes accessed | tf_op | source)
XLA Modules:
  0.0 348.1 jit_solution(3109868991489089546)
XLA Ops:
  7.2 6.2 %shard_map.349 = (bf16[512,384]{1,0:T(8,128)(2,1)}, bf16[512,768]{1,0:T(8,128)(2,1)}, f32[512,128]{1,0:T(8,128)}, f32[512,128]{1,0:T(8,128)}) custom-call(s32[10]{0:T(128)} %stack.65.info, bf16[512,768]{1,0:T(8,128)(2,1)} %tokens.5, bf16[768,384]{1,0:T(8,128)(2,1)} %wq.3, bf16[768,384]{1,0:T(8,128)(2,1)} %wk.3, bf16[768,384]{1,0:T(8,128)(2,1)} %wv.3, ...), custom_call_target="tpu_custom_call" | custom-call | flops 905969664 | bytes 3735552 | tf_op jit(solution)/shard_map/pallas_call | solution.py:519
  13.3 4.9 %collective-permute-start.1 = (bf16[512,768]{1,0:T(8,128)(2,1)}, bf16[512,768]{1,0:T(8,128)(2,1)S(1)}, u32[]{:S(2)}, u32[]{:S(2)}) collective-permute-start(bf16[512,768]{1,0:T(8,128)(2,1)} %get-tuple-element.50.kv_own), channel_id=1, source_target_pairs={{0,4},{2,6},{1,5},{3,7},{8,12},{10,14},{9,13},{11,15},{16,20},{18,... | collective-permute-start | bytes 2359304 | tf_op jit(solution)/shard_map/ppermute | solution.py:545
  18.3 17.0 %collective-permute-done.1.kv_far = bf16[512,768]{1,0:T(8,128)(2,1)S(1)} collective-permute-done((bf16[512,768]{1,0:T(8,128)(2,1)}, bf16[512,768]{1,0:T(8,128)(2,1)S(1)}, u32[]{:S(2)}, u32[]{:S(2)}) %collective-permute-start.1) | collective-permute-done | bytes 786464 | tf_op jit(solution)/shard_map/ppermute | solution.py:545
  35.3 2.3 collective-permute-done.2.kv_cross
  38.5 11.9 %shard_map.350 = (bf16[512,384]{1,0:T(8,128)(2,1)}, f32[384,512]{1,0:T(8,128)}, f32[3,2,512]{2,1,0:T(2,128)}, bf16[512,768]{1,0:T(8,128)(2,1)}) custom-call(s32[10]{0:T(128)} %stack.65.info, bf16[512,384]{1,0:T(8,128)(2,1)} %get-tuple-element.49.q, bf16[512,768]{1,0:T(8,128)(2,1)} %get-tuple-element.50.kv_own, bf16[512,768]{1,0:T(8,128)(2,1)} %copy-done.1, ...), custom_call_target="tpu_custom_call" | custom-call | flops 805306368 | bytes 2359296 | tf_op jit(solution)/shard_map/pallas_call | solution.py:553
  50.4 1.6 collective-permute-start.3
  53.3 9.9 %collective-permute-done.3.other = bf16[512,768]{1,0:T(8,128)(2,1)S(1)} collective-permute-done((bf16[512,768]{1,0:T(8,128)(2,1)}, bf16[512,768]{1,0:T(8,128)(2,1)S(1)}, u32[]{:S(2)}, u32[]{:S(2)}) %collective-permute-start.3) | collective-permute-done | bytes 786464 | tf_op jit(solution)/shard_map/ppermute | solution.py:464
  64.1 9.7 %shard_map.351 = (f32[512,768]{1,0:T(8,128)}, f32[512,1]{1,0:T(8,128)}, bf16[512,768]{1,0:T(8,128)(2,1)}, bf16[512,1536]{1,0:T(8,128)(2,1)}, bf16[512,1536]{1,0:T(8,128)(2,1)}, /*index=5*/bf16[512,768]{1,0:T(8,128)(2,1)}) custom-call(bf16[512,768]{1,0:T(8,128)(2,1)} %tokens.5, bf16[512,768]{1,0:T(8,128)(2,1)} %get-tuple-element.51.part, ...), custom_call_target="tpu_custom_call" | custom-call | flops 2415919104 | bytes 11010048 | tf_op jit(solution)/shard_map/pallas_call | solution.py:585
  73.8 1.6 collective-permute-start.4
  75.4 12.3 %collective-permute-done.4.other = bf16[512,768]{1,0:T(8,128)(2,1)S(1)} collective-permute-done((bf16[512,768]{1,0:T(8,128)(2,1)}, bf16[512,768]{1,0:T(8,128)(2,1)S(1)}, u32[]{:S(2)}, u32[]{:S(2)}) %collective-permute-start.4) | collective-permute-done | bytes 786464 | tf_op jit(solution)/shard_map/ppermute | solution.py:464
  88.6 11.5 %shard_map.352 = (bf16[512,768]{1,0:T(8,128)(2,1)}, bf16[512,768]{1,0:T(8,128)(2,1)}, bf16[512,1536]{1,0:T(8,128)(2,1)}, bf16[512,768]{1,0:T(8,128)(2,1)}, f32[5...) custom-call(f32[512,768]{1,0:T(8,128)} %get-tuple-element.52.normed_first.normed, ...), custom_call_target="tpu_custom_call" | custom-call | flops 2415919104 | bytes 11010048 | tf_op jit(solution)/shard_map/pallas_call | solution.py:608
  100.1 1.6 collective-permute-start.5
  103.0 6.4 %collective-permute-start.6 = (bf16[512,384]{1,0:T(8,128)(2,1)S(1)}, bf16[512,384]{1,0:T(8,128)(2,1)}, u32[]{:S(2)}, u32[]{:S(2)}) collective-permute-start(bf16[512,384]{1,0:T(8,128)(2,1)S(1)} %copy-done.5), channel_id=1, source_target_pairs={{0,2},{2,0},{4,6},{6,4},{1,3},{3,1},{5,7},{7,5},{8,10},{10,8},{12,... | collective-permute-start | bytes 1179656 | tf_op jit(solution)/shard_map/ppermute | solution.py:464
  109.4 6.1 %collective-permute-done.7.q_far = bf16[512,384]{1,0:T(8,128)(2,1)S(1)} collective-permute-done((bf16[512,384]{1,0:T(8,128)(2,1)S(1)}, bf16[512,384]{1,0:T(8,128)(2,1)S(1)}, u32[]{:S(2)}, u32[]{:S(2)}) %collective-permute-start.7) | collective-permute-done | bytes 393248 | tf_op jit(solution)/shard_map/ppermute | solution.py:545
  115.5 5.4 %collective-permute-start.8 = (bf16[512,384]{1,0:T(8,128)(2,1)S(1)}, bf16[512,384]{1,0:T(8,128)(2,1)}, u32[]{:S(2)}, u32[]{:S(2)}) collective-permute-start(bf16[512,384]{1,0:T(8,128)(2,1)S(1)} %collective-permute-done.7.q_far), channel_id=1, source_target_pairs={{0,2},{2,0},{4,6},{6,4},{1,3},{3,1},{5,7},{7,5},{8,10},{10,8},{12,... | collective-permute-start | bytes 1179656 | tf_op jit(solution)/shard_map/ppermute | solution.py:464
  121.8 5.6 %shard_map.353 = (f32[512,768]{1,0:T(8,128)}, bf16[512,768]{1,0:T(8,128)(2,1)}, bf16[512,384]{1,0:T(8,128)(2,1)}, f32[3,2,512]{2,1,0:T(2,128)}, f32[8,768]{1,0:T(8,128)}) custom-call(f32[512,768]{1,0:T(8,128)} %get-tuple-element.56.res_second, bf16[512,768]{1,0:T(8,128)(2,1)} %get-tuple-element.57.part, bf16[512,768]{1,0:T(8,128)(2,1)} %copy-done.7, ...), custom_call_target="tpu_custom_call" | custom-call | flops 603979776 | bytes 7864320 | tf_op jit(solution)/shard_map/pallas_call | solution.py:636
  127.4 1.8 convolution_convert_fusion.2
  129.4 1.4 convolution_convert_fusion.1
  133.8 6.0 %collective-permute-start.40 = (bf16[96,768]{1,0:T(8,128)(2,1)}, bf16[96,768]{1,0:T(8,128)(2,1)}, u32[]{:S(2)}, u32[]{:S(2)}) collective-permute-start(bf16[96,768]{1,0:T(8,128)(2,1)} %constant_dynamic-slice_fusion.10), channel_id=1, source_target_pairs={{0,4},{2,6},{4,0},{6,2},{1,5},{3,7},{5,1},{7,3},{8,12},{10,14},{12... | collective-permute-start | bytes 442376 | tf_op jit(solution)/shard_map/ppermute | solution.py:464
  139.8 1.4 convolution_convert_fusion
  141.7 2.9 collective-permute-done.40
  145.6 5.2 %collective-permute-start.41 = (bf16[48,768]{1,0:T(8,128)(2,1)S(1)}, bf16[48,768]{1,0:T(8,128)(2,1)S(1)}, u32[]{:S(2)}, u32[]{:S(2)}) collective-permute-start(bf16[48,768]{1,0:T(8,128)(2,1)S(1)} %constant_dynamic-slice_fusion.9), channel_id=1, source_target_pairs={{0,8},{8,0},{16,24},{24,16},{1,9},{9,1},{17,25},{25,17},{2,10},{10... | collective-permute-start | bytes 221192 | tf_op jit(solution)/shard_map/ppermute | solution.py:464
  150.8 1.6 add_convert_fusion.1
  152.4 1.4 collective-permute-done.41
  155.1 2.8 collective-permute-start.42
  158.3 8.3 %collective-permute-done.10.grad_far = bf16[512,384]{1,0:T(8,128)(2,1)S(1)} collective-permute-done((bf16[512,384]{1,0:T(8,128)(2,1)S(1)}, bf16[512,384]{1,0:T(8,128)(2,1)S(1)}, u32[]{:S(2)}, u32[]{:S(2)}) %collective-permute-start.10) | collective-permute-done | bytes 393248 | tf_op jit(solution)/shard_map/ppermute | solution.py:545
  166.6 2.6 collective-permute-start.43
  169.3 2.3 collective-permute-done.43
  174.2 1.6 collective-permute-start.44
  179.1 1.6 collective-permute-start.48
  180.7 2.3 collective-permute-start.56
  184.0 35.2 %shard_map.354 = (bf16[768,384]{1,0:T(8,128)(2,1)}, bf16[768,384]{1,0:T(8,128)(2,1)}, bf16[768,384]{1,0:T(8,128)(2,1)}, f32[8,384]{1,0:T(8,128)}, bf16[512,768]{1,0:T(8,128)(2,1)}) custom-call(s32[10]{0:T(128)} %stack.65.info, bf16[512,384]{1,0:T(8,128)(2,1)} %get-tuple-element.49.q, bf16[512,384]{1,0:T(8,128)(2,1)} %get-tuple-element.61.grad, ...), custom_call_target="tpu_custom_call" | custom-call | flops 2013265920 | bytes 7864320 | tf_op jit(solution)/shard_map/pallas_call | solution.py:660
  219.3 1.6 collective-permute-start.18
  222.0 7.2 %collective-permute-start.27 = (f32[16,768]{1,0:T(8,128)S(1)}, f32[16,768]{1,0:T(8,128)S(1)}, u32[]{:S(2)}, u32[]{:S(2)}) collective-permute-start(f32[16,768]{1,0:T(8,128)S(1)} %pad.9), channel_id=1, source_target_pairs={{0,2},{2,0},{4,6},{6,4},{1,3},{3,1},{5,7},{7,5},{8,10},{10,8},{12,... | collective-permute-start | bytes 147464 | tf_op jit(solution)/shard_map/ppermute | solution.py:464
  230.4 4.0 %collective-permute-done.28 = f32[16,768]{1,0:T(8,128)S(1)} collective-permute-done((f32[16,768]{1,0:T(8,128)S(1)}, f32[16,768]{1,0:T(8,128)S(1)}, u32[]{:S(2)}, u32[]{:S(2)}) %collective-permute-start.28) | collective-permute-done | bytes 49184 | tf_op jit(solution)/shard_map/ppermute | solution.py:464
  235.7 2.9 collective-permute-done.29
  239.3 1.4 collective-permute-start.30
  242.6 2.5 collective-permute-done.30
  247.8 2.1 collective-permute-start.32
  251.1 2.2 fusion.3
  253.3 2.7 collective-permute-done.32
  257.0 6.3 %collective-permute-start.33 = (bf16[96,384]{1,0:T(8,128)(2,1)S(1)}, bf16[96,384]{1,0:T(8,128)(2,1)S(1)}, u32[]{:S(2)}, u32[]{:S(2)}) collective-permute-start(bf16[96,384]{1,0:T(8,128)(2,1)S(1)} %constant_dynamic-slice_fusion.13), channel_id=1, source_target_pairs={{0,16},{8,24},{16,0},{24,8},{1,17},{9,25},{17,1},{25,9},{2,18},{10... | collective-permute-start | bytes 221192 | tf_op jit(solution)/shard_map/ppermute | solution.py:464
  264.4 1.6 collective-permute-start.50
  267.3 3.0 collective-permute-start.58
  275.2 2.0 collective-permute-done.58
  278.0 4.2 %collective-permute-done.20 = bf16[192,768]{1,0:T(8,128)(2,1)S(1)} collective-permute-done((bf16[192,768]{1,0:T(8,128)(2,1)S(1)}, bf16[192,768]{1,0:T(8,128)(2,1)S(1)}, u32[]{:S(2)}, u32[]{:S(2)}) %collective-permute-start.20) | collective-permute-done | bytes 294944 | tf_op jit(solution)/shard_map/ppermute | solution.py:464
  282.4 1.4 collective-permute-done.51
  283.8 1.6 collective-permute-start.52
  285.4 3.0 collective-permute-done.59
  288.4 2.3 collective-permute-start.60
  290.7 1.8 collective-permute-done.21
  292.5 2.2 collective-permute-start.22
  294.7 4.2 %collective-permute-done.52 = bf16[96,1536]{1,0:T(8,128)(2,1)S(1)} collective-permute-done((bf16[96,1536]{1,0:T(8,128)(2,1)S(1)}, bf16[96,1536]{1,0:T(8,128)(2,1)S(1)}, u32[]{:S(2)}, u32[]{:S(2)}) %collective-permute-start.52) | collective-permute-done | bytes 294944 | tf_op jit(solution)/shard_map/ppermute | solution.py:464
  299.2 1.6 collective-permute-done.22
  302.1 1.8 collective-permute-start.36
  303.9 10.6 %collective-permute-done.23 = bf16[48,768]{1,0:T(8,128)(2,1)S(1)} collective-permute-done((bf16[48,768]{1,0:T(8,128)(2,1)S(1)}, bf16[48,768]{1,0:T(8,128)(2,1)S(1)}, u32[]{:S(2)}, u32[]{:S(2)}) %collective-permute-start.23) | collective-permute-done | bytes 73760 | tf_op jit(solution)/shard_map/ppermute | solution.py:464
  316.9 1.9 collective-permute-start.61
  318.8 2.5 collective-permute-done.24
  321.4 2.0 collective-permute-start.25
  324.5 10.5 %collective-permute-done.25 = bf16[192,768]{1,0:T(8,128)(2,1)S(1)} collective-permute-done((bf16[192,768]{1,0:T(8,128)(2,1)S(1)}, bf16[192,768]{1,0:T(8,128)(2,1)S(1)}, u32[]{:S(2)}, u32[]{:S(2)}) %collective-permute-start.25) | collective-permute-done | bytes 294944 | tf_op jit(solution)/shard_map/ppermute | solution.py:464
  336.9 2.3 add_convert_fusion.2
  340.8 1.6 slice_convert_fusion
  342.3 2.9 fusion
  345.2 2.7 fusion.1
  (248 shorter events, 52.2 us)
Async XLA Ops:
  13.3 21.9 %collective-permute-start.1 = (bf16[512,768]{1,0:T(8,128)(2,1)}, bf16[512,768]{1,0:T(8,128)(2,1)S(1)}, u32[]{:S(2)}, u32[]{:S(2)}) collective-permute-start(bf16[512,768]{1,0:T(8,128)(2,1)} %get-tuple-element.50.kv_own), channel_id=1, source_target_pairs={{0,4},{2,6},{1,5},{3,7},{8,12},{10,14},{9,13},{11,15},{16,20},{18,... | collective-permute-start | bytes 2359304 | tf_op jit(solution)/shard_map/ppermute | solution.py:545
  18.2 17.1 %collective-permute-start = (bf16[512,768]{1,0:T(8,128)(2,1)}, bf16[512,768]{1,0:T(8,128)(2,1)S(1)}, u32[]{:S(2)}, u32[]{:S(2)}) collective-permute-start(bf16[512,768]{1,0:T(8,128)(2,1)} %get-tuple-element.50.kv_own), channel_id=1, source_target_pairs={{0,2},{2,0},{4,6},{6,4},{1,3},{3,1},{5,7},{7,5},{8,10},{10,8},{12,... | collective-permute-start | bytes 2359304 | tf_op jit(solution)/shard_map/ppermute | solution.py:464
  35.3 2.3 collective-permute-start.2
  50.4 12.8 %collective-permute-start.3 = (bf16[512,768]{1,0:T(8,128)(2,1)}, bf16[512,768]{1,0:T(8,128)(2,1)S(1)}, u32[]{:S(2)}, u32[]{:S(2)}) collective-permute-start(bf16[512,768]{1,0:T(8,128)(2,1)} %get-tuple-element.51.part), channel_id=1, source_target_pairs={{0,1},{1,0},{2,3},{3,2},{4,5},{5,4},{6,7},{7,6},{8,9},{9,8},{10,11... | collective-permute-start | bytes 2359304 | tf_op jit(solution)/shard_map/ppermute | solution.py:464
  73.8 13.9 %collective-permute-start.4 = (bf16[512,768]{1,0:T(8,128)(2,1)}, bf16[512,768]{1,0:T(8,128)(2,1)S(1)}, u32[]{:S(2)}, u32[]{:S(2)}) collective-permute-start(bf16[512,768]{1,0:T(8,128)(2,1)} %get-tuple-element.53.part), channel_id=1, source_target_pairs={{0,1},{1,0},{2,3},{3,2},{4,5},{5,4},{6,7},{7,6},{8,9},{9,8},{10,11... | collective-permute-start | bytes 2359304 | tf_op jit(solution)/shard_map/ppermute | solution.py:464
  100.1 20.8 %collective-permute-start.5 = (bf16[512,768]{1,0:T(8,128)(2,1)}, bf16[512,768]{1,0:T(8,128)(2,1)S(1)}, u32[]{:S(2)}, u32[]{:S(2)}) collective-permute-start(bf16[512,768]{1,0:T(8,128)(2,1)} %get-tuple-element.57.part), channel_id=1, source_target_pairs={{0,1},{1,0},{2,3},{3,2},{4,5},{5,4},{6,7},{7,6},{8,9},{9,8},{10,11... | collective-permute-start | bytes 2359304 | tf_op jit(solution)/shard_map/ppermute | solution.py:464
  101.7 13.8 %collective-permute-start.7 = (bf16[512,384]{1,0:T(8,128)(2,1)S(1)}, bf16[512,384]{1,0:T(8,128)(2,1)S(1)}, u32[]{:S(2)}, u32[]{:S(2)}) collective-permute-start(bf16[512,384]{1,0:T(8,128)(2,1)S(1)} %copy-done.5), channel_id=1, source_target_pairs={{4,0},{6,2},{5,1},{7,3},{12,8},{14,10},{13,9},{15,11},{20,16},{22,... | collective-permute-start | bytes 1179656 | tf_op jit(solution)/shard_map/ppermute | solution.py:545
  103.0 68.6 %collective-permute-start.6 = (bf16[512,384]{1,0:T(8,128)(2,1)S(1)}, bf16[512,384]{1,0:T(8,128)(2,1)}, u32[]{:S(2)}, u32[]{:S(2)}) collective-permute-start(bf16[512,384]{1,0:T(8,128)(2,1)S(1)} %copy-done.5), channel_id=1, source_target_pairs={{0,2},{2,0},{4,6},{6,4},{1,3},{3,1},{5,7},{7,5},{8,10},{10,8},{12,... | collective-permute-start | bytes 1179656 | tf_op jit(solution)/shard_map/ppermute | solution.py:464
  115.5 57.4 %collective-permute-start.8 = (bf16[512,384]{1,0:T(8,128)(2,1)S(1)}, bf16[512,384]{1,0:T(8,128)(2,1)}, u32[]{:S(2)}, u32[]{:S(2)}) collective-permute-start(bf16[512,384]{1,0:T(8,128)(2,1)S(1)} %collective-permute-done.7.q_far), channel_id=1, source_target_pairs={{0,2},{2,0},{4,6},{6,4},{1,3},{3,1},{5,7},{7,5},{8,10},{10,8},{12,... | collective-permute-start | bytes 1179656 | tf_op jit(solution)/shard_map/ppermute | solution.py:464
  129.3 3.8 %collective-permute-start.39 = (bf16[192,768]{1,0:T(8,128)(2,1)S(1)}, bf16[192,768]{1,0:T(8,128)(2,1)S(1)}, u32[]{:S(2)}, u32[]{:S(2)}) collective-permute-start(bf16[192,768]{1,0:T(8,128)(2,1)S(1)} %constant_dynamic-slice_fusion.11), channel_id=1, source_target_pairs={{0,2},{2,0},{4,6},{6,4},{1,3},{3,1},{5,7},{7,5},{8,10},{10,8},{12,... | collective-permute-start | bytes 884744 | tf_op jit(solution)/shard_map/ppermute | solution.py:464
  132.6 13.0 %collective-permute-start.47 = (bf16[384,1536]{1,0:T(8,128)(2,1)}, bf16[384,1536]{1,0:T(8,128)(2,1)}, u32[]{:S(2)}, u32[]{:S(2)}) collective-permute-start(bf16[384,1536]{1,0:T(8,128)(2,1)} %constant_dynamic-slice_fusion.7), channel_id=1, source_target_pairs={{0,2},{2,0},{4,6},{6,4},{1,3},{3,1},{5,7},{7,5},{8,10},{10,8},{12,... | collective-permute-start | bytes 3538952 | tf_op jit(solution)/shard_map/ppermute | solution.py:464
  133.8 10.8 %collective-permute-start.40 = (bf16[96,768]{1,0:T(8,128)(2,1)}, bf16[96,768]{1,0:T(8,128)(2,1)}, u32[]{:S(2)}, u32[]{:S(2)}) collective-permute-start(bf16[96,768]{1,0:T(8,128)(2,1)} %constant_dynamic-slice_fusion.10), channel_id=1, source_target_pairs={{0,4},{2,6},{4,0},{6,2},{1,5},{3,7},{5,1},{7,3},{8,12},{10,14},{12... | collective-permute-start | bytes 442376 | tf_op jit(solution)/shard_map/ppermute | solution.py:464
  141.4 13.7 %collective-permute-start.55 = (bf16[768,768]{1,0:T(8,128)(2,1)S(1)}, bf16[768,768]{1,0:T(8,128)(2,1)S(1)}, u32[]{:S(2)}, u32[]{:S(2)}) collective-permute-start(bf16[768,768]{1,0:T(8,128)(2,1)S(1)} %constant_dynamic-slice_fusion.3), channel_id=1, source_target_pairs={{0,2},{2,0},{4,6},{6,4},{1,3},{3,1},{5,7},{7,5},{8,10},{10,8},{12,... | collective-permute-start | bytes 3538952 | tf_op jit(solution)/shard_map/ppermute | solution.py:464
  144.6 38.5 %collective-permute-start.9 = (bf16[512,384]{1,0:T(8,128)(2,1)S(1)}, bf16[512,384]{1,0:T(8,128)(2,1)S(1)}, u32[]{:S(2)}, u32[]{:S(2)}) collective-permute-start(bf16[512,384]{1,0:T(8,128)(2,1)S(1)} %copy-done.13), channel_id=1, source_target_pairs={{0,2},{2,0},{4,6},{6,4},{1,3},{3,1},{5,7},{7,5},{8,10},{10,8},{12,... | collective-permute-start | bytes 1179656 | tf_op jit(solution)/shard_map/ppermute | solution.py:464
  145.6 8.2 %collective-permute-start.41 = (bf16[48,768]{1,0:T(8,128)(2,1)S(1)}, bf16[48,768]{1,0:T(8,128)(2,1)S(1)}, u32[]{:S(2)}, u32[]{:S(2)}) collective-permute-start(bf16[48,768]{1,0:T(8,128)(2,1)S(1)} %constant_dynamic-slice_fusion.9), channel_id=1, source_target_pairs={{0,8},{8,0},{16,24},{24,16},{1,9},{9,1},{17,25},{25,17},{2,10},{10... | collective-permute-start | bytes 221192 | tf_op jit(solution)/shard_map/ppermute | solution.py:464
  153.8 12.8 %collective-permute-start.10 = (bf16[512,384]{1,0:T(8,128)(2,1)S(1)}, bf16[512,384]{1,0:T(8,128)(2,1)S(1)}, u32[]{:S(2)}, u32[]{:S(2)}) collective-permute-start(bf16[512,384]{1,0:T(8,128)(2,1)S(1)} %copy-done.13), channel_id=1, source_target_pairs={{4,0},{6,2},{5,1},{7,3},{12,8},{14,10},{13,9},{15,11},{20,16},{22,... | collective-permute-start | bytes 1179656 | tf_op jit(solution)/shard_map/ppermute | solution.py:545
  155.1 11.5 %collective-permute-start.42 = (bf16[24,768]{1,0:T(8,128)(2,1)S(1)}, bf16[24,768]{1,0:T(8,128)(2,1)S(1)}, u32[]{:S(2)}, u32[]{:S(2)}) collective-permute-start(bf16[24,768]{1,0:T(8,128)(2,1)S(1)} %constant_dynamic-slice_fusion.8), channel_id=1, source_target_pairs={{0,16},{8,24},{16,0},{24,8},{1,17},{9,25},{17,1},{25,9},{2,18},{10... | collective-permute-start | bytes 110600 | tf_op jit(solution)/shard_map/ppermute | solution.py:464
  158.3 14.6 %copy-start.18 = (f32[3,2,512]{2,1,0:T(2,128)S(1)}, f32[3,2,512]{2,1,0:T(2,128)}, u32[]{:S(2)}) copy-start(f32[3,2,512]{2,1,0:T(2,128)} %get-tuple-element.63.rowdot) | copy-start | bytes 36868
  166.6 16.5 %collective-permute-start.11 = (bf16[512,384]{1,0:T(8,128)(2,1)S(1)}, bf16[512,384]{1,0:T(8,128)(2,1)S(1)}, u32[]{:S(2)}, u32[]{:S(2)}) collective-permute-start(bf16[512,384]{1,0:T(8,128)(2,1)S(1)} %collective-permute-done.10.grad_far), channel_id=1, source_target_pairs={{0,2},{2,0},{4,6},{6,4},{1,3},{3,1},{5,7},{7,5},{8,10},{10,8},{12,... | collective-permute-start | bytes 1179656 | tf_op jit(solution)/shard_map/ppermute | solution.py:464
  166.6 4.9 %collective-permute-start.43 = (bf16[24,768]{1,0:T(8,128)(2,1)S(1)}, bf16[24,768]{1,0:T(8,128)(2,1)S(1)}, u32[]{:S(2)}, u32[]{:S(2)}) collective-permute-start(bf16[24,768]{1,0:T(8,128)(2,1)S(1)} %add_convert_fusion.19), channel_id=1, source_target_pairs={{0,16},{8,24},{16,0},{24,8},{1,17},{9,25},{17,1},{25,9},{2,18},{10... | collective-permute-start | bytes 110600 | tf_op jit(solution)/shard_map/ppermute | solution.py:464
  171.6 2.7 collective-permute-start.12
  171.6 5.6 %collective-permute-start.13 = (f32[3,2,512]{2,1,0:T(2,128)S(1)}, f32[3,2,512]{2,1,0:T(2,128)S(1)}, u32[]{:S(2)}, u32[]{:S(2)}) collective-permute-start(f32[3,2,512]{2,1,0:T(2,128)S(1)} %copy-done.17), channel_id=1, source_target_pairs={{4,0},{6,2},{5,1},{7,3},{12,8},{14,10},{13,9},{15,11},{20,16},{22,... | collective-permute-start | bytes 36872 | tf_op jit(solution)/shard_map/ppermute | solution.py:545
  172.9 5.6 %collective-permute-start.16 = (f32[3,2,512]{2,1,0:T(2,128)S(1)}, f32[3,2,512]{2,1,0:T(2,128)S(1)}, u32[]{:S(2)}, u32[]{:S(2)}) collective-permute-start(f32[3,2,512]{2,1,0:T(2,128)S(1)} %copy-done.18), channel_id=1, source_target_pairs={{4,0},{6,2},{5,1},{7,3},{12,8},{14,10},{13,9},{15,11},{20,16},{22,... | collective-permute-start | bytes 36872 | tf_op jit(solution)/shard_map/ppermute | solution.py:545
  174.2 4.7 %collective-permute-start.44 = (bf16[48,768]{1,0:T(8,128)(2,1)S(1)}, bf16[48,768]{1,0:T(8,128)(2,1)S(1)}, u32[]{:S(2)}, u32[]{:S(2)}) collective-permute-start(bf16[48,768]{1,0:T(8,128)(2,1)S(1)} %maximum_select_fusion.19), channel_id=1, source_target_pairs={{0,8},{8,0},{16,24},{24,16},{1,9},{9,1},{17,25},{25,17},{2,10},{10... | collective-permute-start | bytes 221192 | tf_op jit(solution)/shard_map/ppermute | solution.py:464
  177.2 1.9 collective-permute-start.14
  178.5 2.2 collective-permute-start.15
  179.0 4.0 %collective-permute-start.17 = (f32[3,2,512]{2,1,0:T(2,128)S(1)}, f32[3,2,512]{2,1,0:T(2,128)S(1)}, u32[]{:S(2)}, u32[]{:S(2)}) collective-permute-start(f32[3,2,512]{2,1,0:T(2,128)S(1)} %collective-permute-done.16.rowdot_far), channel_id=1, source_target_pairs={{0,2},{2,0},{4,6},{6,4},{1,3},{3,1},{5,7},{7,5},{8,10},{10,8},{12,... | collective-permute-start | bytes 36872 | tf_op jit(solution)/shard_map/ppermute | solution.py:464
  179.1 59.5 %collective-permute-start.48 = (bf16[192,1536]{1,0:T(8,128)(2,1)S(1)}, bf16[192,1536]{1,0:T(8,128)(2,1)S(1)}, u32[]{:S(2)}, u32[]{:S(2)}) collective-permute-start(bf16[192,1536]{1,0:T(8,128)(2,1)S(1)} %constant_dynamic-slice_fusion.6), channel_id=1, source_target_pairs={{0,8},{8,0},{16,24},{24,16},{1,9},{9,1},{17,25},{25,17},{2,10},{10... | collective-permute-start | bytes 1769480 | tf_op jit(solution)/shard_map/ppermute | solution.py:464
  180.7 58.6 %collective-permute-start.56 = (bf16[384,768]{1,0:T(8,128)(2,1)S(1)}, bf16[384,768]{1,0:T(8,128)(2,1)}, u32[]{:S(2)}, u32[]{:S(2)}) collective-permute-start(bf16[384,768]{1,0:T(8,128)(2,1)S(1)} %constant_dynamic-slice_fusion.2), channel_id=1, source_target_pairs={{0,4},{2,6},{4,0},{6,2},{1,5},{3,7},{5,1},{7,3},{8,12},{10,14},{12... | collective-permute-start | bytes 1769480 | tf_op jit(solution)/shard_map/ppermute | solution.py:464
  183.0 51.3 %collective-permute-start.45 = (bf16[96,768]{1,0:T(8,128)(2,1)S(1)}, bf16[96,768]{1,0:T(8,128)(2,1)S(1)}, u32[]{:S(2)}, u32[]{:S(2)}) collective-permute-start(bf16[96,768]{1,0:T(8,128)(2,1)S(1)} %maximum_select_fusion.17), channel_id=1, source_target_pairs={{0,4},{2,6},{4,0},{6,2},{1,5},{3,7},{5,1},{7,3},{8,12},{10,14},{12... | collective-permute-start | bytes 442376 | tf_op jit(solution)/shard_map/ppermute | solution.py:464
  219.3 117.1 %collective-permute-start.18 = (bf16[512,768]{1,0:T(8,128)(2,1)}, bf16[512,768]{1,0:T(8,128)(2,1)}, u32[]{:S(2)}, u32[]{:S(2)}) collective-permute-start(bf16[512,768]{1,0:T(8,128)(2,1)} %get-tuple-element.66), channel_id=1, source_target_pairs={{0,1},{1,0},{2,3},{3,2},{4,5},{5,4},{6,7},{7,6},{8,9},{9,8},{10,11... | collective-permute-start | bytes 2359304 | tf_op jit(solution)/shard_map/ppermute | solution.py:464
  222.0 8.1 %collective-permute-start.27 = (f32[16,768]{1,0:T(8,128)S(1)}, f32[16,768]{1,0:T(8,128)S(1)}, u32[]{:S(2)}, u32[]{:S(2)}) collective-permute-start(f32[16,768]{1,0:T(8,128)S(1)} %pad.9), channel_id=1, source_target_pairs={{0,2},{2,0},{4,6},{6,4},{1,3},{3,1},{5,7},{7,5},{8,10},{10,8},{12,... | collective-permute-start | bytes 147464 | tf_op jit(solution)/shard_map/ppermute | solution.py:464
  230.2 4.2 %collective-permute-start.28 = (f32[16,768]{1,0:T(8,128)S(1)}, f32[16,768]{1,0:T(8,128)S(1)}, u32[]{:S(2)}, u32[]{:S(2)}) collective-permute-start(f32[16,768]{1,0:T(8,128)S(1)} %pad_add_fusion), channel_id=1, source_target_pairs={{0,4},{2,6},{4,0},{6,2},{1,5},{3,7},{5,1},{7,3},{8,12},{10,14},{12... | collective-permute-start | bytes 147464 | tf_op jit(solution)/shard_map/ppermute | solution.py:464
  234.3 37.4 %collective-permute-start.19 = (bf16[384,768]{1,0:T(8,128)(2,1)S(1)}, bf16[384,768]{1,0:T(8,128)(2,1)}, u32[]{:S(2)}, u32[]{:S(2)}) collective-permute-start(bf16[384,768]{1,0:T(8,128)(2,1)S(1)} %constant_dynamic-slice_fusion.19), channel_id=1, source_target_pairs={{0,2},{2,0},{4,6},{6,4},{1,3},{3,1},{5,7},{7,5},{8,10},{10,8},{12,... | collective-permute-start | bytes 1769480 | tf_op jit(solution)/shard_map/ppermute | solution.py:464
  234.3 4.2 %collective-permute-start.29 = (f32[16,768]{1,0:T(8,128)S(1)}, f32[16,768]{1,0:T(8,128)S(1)}, u32[]{:S(2)}, u32[]{:S(2)}) collective-permute-start(f32[16,768]{1,0:T(8,128)S(1)} %add.174), channel_id=1, source_target_pairs={{0,8},{8,0},{16,24},{24,16},{1,9},{9,1},{17,25},{25,17},{2,10},{10... | collective-permute-start | bytes 147464 | tf_op jit(solution)/shard_map/ppermute | solution.py:464
  238.6 8.5 %collective-permute-start.31 = (bf16[384,384]{1,0:T(8,128)(2,1)S(1)}, bf16[384,384]{1,0:T(8,128)(2,1)S(1)}, u32[]{:S(2)}, u32[]{:S(2)}) collective-permute-start(bf16[384,384]{1,0:T(8,128)(2,1)S(1)} %constant_dynamic-slice_fusion.15), channel_id=1, source_target_pairs={{0,2},{2,0},{4,6},{6,4},{1,3},{3,1},{5,7},{7,5},{8,10},{10,8},{12,... | collective-permute-start | bytes 884744 | tf_op jit(solution)/shard_map/ppermute | solution.py:464
  238.6 12.6 %collective-permute-start.46 = (bf16[192,768]{1,0:T(8,128)(2,1)S(1)}, bf16[192,768]{1,0:T(8,128)(2,1)}, u32[]{:S(2)}, u32[]{:S(2)}) collective-permute-start(bf16[192,768]{1,0:T(8,128)(2,1)S(1)} %maximum_select_fusion.12), channel_id=1, source_target_pairs={{0,2},{2,0},{4,6},{6,4},{1,3},{3,1},{5,7},{7,5},{8,10},{10,8},{12,... | collective-permute-start | bytes 884744 | tf_op jit(solution)/shard_map/ppermute | solution.py:464
  239.3 5.8 %collective-permute-start.30 = (f32[16,768]{1,0:T(8,128)S(1)}, f32[16,768]{1,0:T(8,128)S(1)}, u32[]{:S(2)}, u32[]{:S(2)}) collective-permute-start(f32[16,768]{1,0:T(8,128)S(1)} %add.175), channel_id=1, source_target_pairs={{0,16},{8,24},{16,0},{24,8},{1,17},{9,25},{17,1},{25,9},{2,18},{10... | collective-permute-start | bytes 147464 | tf_op jit(solution)/shard_map/ppermute | solution.py:464
  245.1 18.2 %collective-permute-start.49 = (bf16[96,1536]{1,0:T(8,128)(2,1)}, bf16[96,1536]{1,0:T(8,128)(2,1)}, u32[]{:S(2)}, u32[]{:S(2)}) collective-permute-start(bf16[96,1536]{1,0:T(8,128)(2,1)} %constant_dynamic-slice_fusion.5), channel_id=1, source_target_pairs={{0,16},{8,24},{16,0},{24,8},{1,17},{9,25},{17,1},{25,9},{2,18},{10... | collective-permute-start | bytes 884744 | tf_op jit(solution)/shard_map/ppermute | solution.py:464
  247.8 8.2 %collective-permute-start.32 = (bf16[192,384]{1,0:T(8,128)(2,1)}, bf16[192,384]{1,0:T(8,128)(2,1)}, u32[]{:S(2)}, u32[]{:S(2)}) collective-permute-start(bf16[192,384]{1,0:T(8,128)(2,1)} %constant_dynamic-slice_fusion.14), channel_id=1, source_target_pairs={{0,8},{8,0},{16,24},{24,16},{1,9},{9,1},{17,25},{25,17},{2,10},{10... | collective-permute-start | bytes 442376 | tf_op jit(solution)/shard_map/ppermute | solution.py:464
  251.1 15.5 %collective-permute-start.57 = (bf16[192,768]{1,0:T(8,128)(2,1)}, bf16[192,768]{1,0:T(8,128)(2,1)S(1)}, u32[]{:S(2)}, u32[]{:S(2)}) collective-permute-start(bf16[192,768]{1,0:T(8,128)(2,1)} %constant_dynamic-slice_fusion.1), channel_id=1, source_target_pairs={{0,8},{8,0},{16,24},{24,16},{1,9},{9,1},{17,25},{25,17},{2,10},{10... | collective-permute-start | bytes 884744 | tf_op jit(solution)/shard_map/ppermute | solution.py:464
  257.0 9.7 %collective-permute-start.33 = (bf16[96,384]{1,0:T(8,128)(2,1)S(1)}, bf16[96,384]{1,0:T(8,128)(2,1)S(1)}, u32[]{:S(2)}, u32[]{:S(2)}) collective-permute-start(bf16[96,384]{1,0:T(8,128)(2,1)S(1)} %constant_dynamic-slice_fusion.13), channel_id=1, source_target_pairs={{0,16},{8,24},{16,0},{24,8},{1,17},{9,25},{17,1},{25,9},{2,18},{10... | collective-permute-start | bytes 221192 | tf_op jit(solution)/shard_map/ppermute | solution.py:464
  264.4 9.9 %collective-permute-start.50 = (bf16[48,1536]{1,0:T(8,128)(2,1)S(1)}, bf16[48,1536]{1,0:T(8,128)(2,1)S(1)}, u32[]{:S(2)}, u32[]{:S(2)}) collective-permute-start(bf16[48,1536]{1,0:T(8,128)(2,1)S(1)} %constant_dynamic-slice_fusion.4), channel_id=1, source_target_pairs={{0,4},{2,6},{4,0},{6,2},{1,5},{3,7},{5,1},{7,3},{8,12},{10,14},{12... | collective-permute-start | bytes 442376 | tf_op jit(solution)/shard_map/ppermute | solution.py:464
  266.8 4.0 %collective-permute-start.34 = (bf16[48,384]{1,0:T(8,128)(2,1)S(1)}, bf16[48,384]{1,0:T(8,128)(2,1)S(1)}, u32[]{:S(2)}, u32[]{:S(2)}) collective-permute-start(bf16[48,384]{1,0:T(8,128)(2,1)S(1)} %constant_dynamic-slice_fusion.12), channel_id=1, source_target_pairs={{0,4},{2,6},{4,0},{6,2},{1,5},{3,7},{5,1},{7,3},{8,12},{10,14},{12... | collective-permute-start | bytes 110600 | tf_op jit(solution)/shard_map/ppermute | solution.py:464
  267.3 9.9 %collective-permute-start.58 = (bf16[96,768]{1,0:T(8,128)(2,1)S(1)}, bf16[96,768]{1,0:T(8,128)(2,1)S(1)}, u32[]{:S(2)}, u32[]{:S(2)}) collective-permute-start(bf16[96,768]{1,0:T(8,128)(2,1)S(1)} %constant_dynamic-slice_fusion), channel_id=1, source_target_pairs={{0,16},{8,24},{16,0},{24,8},{1,17},{9,25},{17,1},{25,9},{2,18},{10... | collective-permute-start | bytes 442376 | tf_op jit(solution)/shard_map/ppermute | solution.py:464
  270.8 31.2 %collective-permute-start.35 = (bf16[48,384]{1,0:T(8,128)(2,1)S(1)}, bf16[48,384]{1,0:T(8,128)(2,1)S(1)}, u32[]{:S(2)}, u32[]{:S(2)}) collective-permute-start(bf16[48,384]{1,0:T(8,128)(2,1)S(1)} %add_convert_fusion.20), channel_id=1, source_target_pairs={{0,4},{2,6},{4,0},{6,2},{1,5},{3,7},{5,1},{7,3},{8,12},{10,14},{12... | collective-permute-start | bytes 110600 | tf_op jit(solution)/shard_map/ppermute | solution.py:464
  272.9 9.2 %collective-permute-start.20 = (bf16[192,768]{1,0:T(8,128)(2,1)S(1)}, bf16[192,768]{1,0:T(8,128)(2,1)S(1)}, u32[]{:S(2)}, u32[]{:S(2)}) collective-permute-start(bf16[192,768]{1,0:T(8,128)(2,1)S(1)} %constant_dynamic-slice_fusion.18), channel_id=1, source_target_pairs={{0,4},{2,6},{4,0},{6,2},{1,5},{3,7},{5,1},{7,3},{8,12},{10,14},{12... | collective-permute-start | bytes 884744 | tf_op jit(solution)/shard_map/ppermute | solution.py:464
  274.3 9.4 %collective-permute-start.51 = (bf16[48,1536]{1,0:T(8,128)(2,1)S(1)}, bf16[48,1536]{1,0:T(8,128)(2,1)S(1)}, u32[]{:S(2)}, u32[]{:S(2)}) collective-permute-start(bf16[48,1536]{1,0:T(8,128)(2,1)S(1)} %add_convert_fusion.12), channel_id=1, source_target_pairs={{0,4},{2,6},{4,0},{6,2},{1,5},{3,7},{5,1},{7,3},{8,12},{10,14},{12... | collective-permute-start | bytes 442376 | tf_op jit(solution)/shard_map/ppermute | solution.py:464
  277.2 11.1 %collective-permute-start.59 = (bf16[96,768]{1,0:T(8,128)(2,1)S(1)}, bf16[96,768]{1,0:T(8,128)(2,1)S(1)}, u32[]{:S(2)}, u32[]{:S(2)}) collective-permute-start(bf16[96,768]{1,0:T(8,128)(2,1)S(1)} %add_convert_fusion.11), channel_id=1, source_target_pairs={{0,16},{8,24},{16,0},{24,8},{1,17},{9,25},{17,1},{25,9},{2,18},{10... | collective-permute-start | bytes 442376 | tf_op jit(solution)/shard_map/ppermute | solution.py:464
  282.3 10.2 %collective-permute-start.21 = (bf16[96,768]{1,0:T(8,128)(2,1)S(1)}, bf16[96,768]{1,0:T(8,128)(2,1)S(1)}, u32[]{:S(2)}, u32[]{:S(2)}) collective-permute-start(bf16[96,768]{1,0:T(8,128)(2,1)S(1)} %constant_dynamic-slice_fusion.17), channel_id=1, source_target_pairs={{0,8},{8,0},{16,24},{24,16},{1,9},{9,1},{17,25},{25,17},{2,10},{10... | collective-permute-start | bytes 442376 | tf_op jit(solution)/shard_map/ppermute | solution.py:464
  283.8 15.2 %collective-permute-start.52 = (bf16[96,1536]{1,0:T(8,128)(2,1)S(1)}, bf16[96,1536]{1,0:T(8,128)(2,1)S(1)}, u32[]{:S(2)}, u32[]{:S(2)}) collective-permute-start(bf16[96,1536]{1,0:T(8,128)(2,1)S(1)} %maximum_select_fusion.13), channel_id=1, source_target_pairs={{0,16},{8,24},{16,0},{24,8},{1,17},{9,25},{17,1},{25,9},{2,18},{10... | collective-permute-start | bytes 884744 | tf_op jit(solution)/shard_map/ppermute | solution.py:464
  288.4 28.4 %collective-permute-start.60 = (bf16[192,768]{1,0:T(8,128)(2,1)S(1)}, bf16[192,768]{1,0:T(8,128)(2,1)S(1)}, u32[]{:S(2)}, u32[]{:S(2)}) collective-permute-start(bf16[192,768]{1,0:T(8,128)(2,1)S(1)} %maximum_select_fusion.14), channel_id=1, source_target_pairs={{0,8},{8,0},{16,24},{24,16},{1,9},{9,1},{17,25},{25,17},{2,10},{10... | collective-permute-start | bytes 884744 | tf_op jit(solution)/shard_map/ppermute | solution.py:464
  292.5 8.2 %collective-permute-start.22 = (bf16[48,768]{1,0:T(8,128)(2,1)S(1)}, bf16[48,768]{1,0:T(8,128)(2,1)S(1)}, u32[]{:S(2)}, u32[]{:S(2)}) collective-permute-start(bf16[48,768]{1,0:T(8,128)(2,1)S(1)} %constant_dynamic-slice_fusion.16), channel_id=1, source_target_pairs={{0,16},{8,24},{16,0},{24,8},{1,17},{9,25},{17,1},{25,9},{2,18},{10... | collective-permute-start | bytes 221192 | tf_op jit(solution)/shard_map/ppermute | solution.py:464
  299.1 24.3 %collective-permute-start.53 = (bf16[192,1536]{1,0:T(8,128)(2,1)S(1)}, bf16[192,1536]{1,0:T(8,128)(2,1)S(1)}, u32[]{:S(2)}, u32[]{:S(2)}) collective-permute-start(bf16[192,1536]{1,0:T(8,128)(2,1)S(1)} %maximum_select_fusion.8), channel_id=1, source_target_pairs={{0,8},{8,0},{16,24},{24,16},{1,9},{9,1},{17,25},{25,17},{2,10},{10... | collective-permute-start | bytes 1769480 | tf_op jit(solution)/shard_map/ppermute | solution.py:464
  300.8 13.7 %collective-permute-start.23 = (bf16[48,768]{1,0:T(8,128)(2,1)S(1)}, bf16[48,768]{1,0:T(8,128)(2,1)S(1)}, u32[]{:S(2)}, u32[]{:S(2)}) collective-permute-start(bf16[48,768]{1,0:T(8,128)(2,1)S(1)} %add_convert_fusion.18), channel_id=1, source_target_pairs={{0,16},{8,24},{16,0},{24,8},{1,17},{9,25},{17,1},{25,9},{2,18},{10... | collective-permute-start | bytes 221192 | tf_op jit(solution)/shard_map/ppermute | solution.py:464
  302.1 14.0 %collective-permute-start.36 = (bf16[96,384]{1,0:T(8,128)(2,1)S(1)}, bf16[96,384]{1,0:T(8,128)(2,1)S(1)}, u32[]{:S(2)}, u32[]{:S(2)}) collective-permute-start(bf16[96,384]{1,0:T(8,128)(2,1)S(1)} %maximum_select_fusion.18), channel_id=1, source_target_pairs={{0,16},{8,24},{16,0},{24,8},{1,17},{9,25},{17,1},{25,9},{2,18},{10... | collective-permute-start | bytes 221192 | tf_op jit(solution)/shard_map/ppermute | solution.py:464
  314.5 6.8 %collective-permute-start.24 = (bf16[96,768]{1,0:T(8,128)(2,1)S(1)}, bf16[96,768]{1,0:T(8,128)(2,1)S(1)}, u32[]{:S(2)}, u32[]{:S(2)}) collective-permute-start(bf16[96,768]{1,0:T(8,128)(2,1)S(1)} %maximum_select_fusion.15), channel_id=1, source_target_pairs={{0,8},{8,0},{16,24},{24,16},{1,9},{9,1},{17,25},{25,17},{2,10},{10... | collective-permute-start | bytes 442376 | tf_op jit(solution)/shard_map/ppermute | solution.py:464
  316.1 7.7 %collective-permute-start.37 = (bf16[192,384]{1,0:T(8,128)(2,1)S(1)}, bf16[192,384]{1,0:T(8,128)(2,1)S(1)}, u32[]{:S(2)}, u32[]{:S(2)}) collective-permute-start(bf16[192,384]{1,0:T(8,128)(2,1)S(1)} %maximum_select_fusion.16), channel_id=1, source_target_pairs={{0,8},{8,0},{16,24},{24,16},{1,9},{9,1},{17,25},{25,17},{2,10},{10... | collective-permute-start | bytes 442376 | tf_op jit(solution)/shard_map/ppermute | solution.py:464
  316.9 18.4 %collective-permute-start.61 = (bf16[384,768]{1,0:T(8,128)(2,1)S(1)}, bf16[384,768]{1,0:T(8,128)(2,1)S(1)}, u32[]{:S(2)}, u32[]{:S(2)}) collective-permute-start(bf16[384,768]{1,0:T(8,128)(2,1)S(1)} %maximum_select_fusion.9), channel_id=1, source_target_pairs={{0,4},{2,6},{4,0},{6,2},{1,5},{3,7},{5,1},{7,3},{8,12},{10,14},{12... | collective-permute-start | bytes 1769480 | tf_op jit(solution)/shard_map/ppermute | solution.py:464
  321.4 13.7 %collective-permute-start.25 = (bf16[192,768]{1,0:T(8,128)(2,1)S(1)}, bf16[192,768]{1,0:T(8,128)(2,1)S(1)}, u32[]{:S(2)}, u32[]{:S(2)}) collective-permute-start(bf16[192,768]{1,0:T(8,128)(2,1)S(1)} %maximum_select_fusion.10), channel_id=1, source_target_pairs={{0,4},{2,6},{4,0},{6,2},{1,5},{3,7},{5,1},{7,3},{8,12},{10,14},{12... | collective-permute-start | bytes 884744 | tf_op jit(solution)/shard_map/ppermute | solution.py:464
  323.8 18.5 %collective-permute-start.54 = (bf16[384,1536]{1,0:T(8,128)(2,1)S(1)}, bf16[384,1536]{1,0:T(8,128)(2,1)S(1)}, u32[]{:S(2)}, u32[]{:S(2)}) collective-permute-start(bf16[384,1536]{1,0:T(8,128)(2,1)S(1)} %maximum_select_fusion.3), channel_id=1, source_target_pairs={{0,2},{2,0},{4,6},{6,4},{1,3},{3,1},{5,7},{7,5},{8,10},{10,8},{12,... | collective-permute-start | bytes 3538952 | tf_op jit(solution)/shard_map/ppermute | solution.py:464
  324.0 15.2 %collective-permute-start.38 = (bf16[384,384]{1,0:T(8,128)(2,1)S(1)}, bf16[384,384]{1,0:T(8,128)(2,1)S(1)}, u32[]{:S(2)}, u32[]{:S(2)}) collective-permute-start(bf16[384,384]{1,0:T(8,128)(2,1)S(1)} %maximum_select_fusion.11), channel_id=1, source_target_pairs={{0,2},{2,0},{4,6},{6,4},{1,3},{3,1},{5,7},{7,5},{8,10},{10,8},{12,... | collective-permute-start | bytes 884744 | tf_op jit(solution)/shard_map/ppermute | solution.py:464
  335.3 5.0 %collective-permute-start.26 = (bf16[384,768]{1,0:T(8,128)(2,1)S(1)}, bf16[384,768]{1,0:T(8,128)(2,1)S(1)}, u32[]{:S(2)}, u32[]{:S(2)}) collective-permute-start(bf16[384,768]{1,0:T(8,128)(2,1)S(1)} %maximum_select_fusion.5), channel_id=1, source_target_pairs={{0,2},{2,0},{4,6},{6,4},{1,3},{3,1},{5,7},{7,5},{8,10},{10,8},{12,... | collective-permute-start | bytes 1769480 | tf_op jit(solution)/shard_map/ppermute | solution.py:464
  335.8 9.4 %collective-permute-start.62 = (bf16[768,768]{1,0:T(8,128)(2,1)S(1)}, bf16[768,768]{1,0:T(8,128)(2,1)S(1)}, u32[]{:S(2)}, u32[]{:S(2)}) collective-permute-start(bf16[768,768]{1,0:T(8,128)(2,1)S(1)} %maximum_select_fusion.4), channel_id=1, source_target_pairs={{0,2},{2,0},{4,6},{6,4},{1,3},{3,1},{5,7},{7,5},{8,10},{10,8},{12,... | collective-permute-start | bytes 3538952 | tf_op jit(solution)/shard_map/ppermute | solution.py:464
  (41 other events, 242.9 us)
